TPU v7x, 512 devices: a whole 4x8x8 slice. The times are simulated.
512 devices in a mesh: lon: 64 (over x, z_lo, y), lat: 8 (over z_hi, core).
Axes of the slice: x: 4, y: 8, z: 8 (z_hi: 4, z_lo: 2; z = z_hi * 2 + z_lo), core: 2. Of those that a mesh axis runs over, the one named last changes fastest.
Arguments:
- tokens: bfloat16 [1536, 48, 4, 512], P('lon', 'lat'), may hold values from -48 to 48
- cotangent: bfloat16 [1536, 48, 4, 512], P('lon', 'lat'), may hold values from -6 to 6
- w_qkv: bfloat16 [512, 1536], replicated, may hold values from -0.25 to 0.25
- w_out: bfloat16 [512, 512], replicated, may hold values from -0.25 to 0.25
Outputs:
- grad_tokens: bfloat16 [1536, 48, 4, 512], P('lon', 'lat')
- grad_qkv: float32 [786432], P(('lon', 'lat'))
- grad_out: float32 [262144], P(('lon', 'lat'))
All inputs are finite; a program needn't handle non-finite values.
Results may differ from a plain program's by a relative error of at most 0.022.
The roundings to bfloat16 on the way count: a program that leaves them out, or rounds other values in their place, can miss the bound.
Values may be sent and summed in bfloat16 or wider, within the bound.
A program may use at most 64 MiB of HBM per device.

v0:
```python
import math

import jax
import jax.numpy as jnp
from jax import lax
from jax.sharding import PartitionSpec as P

D = 512
H = 16
E = 32
WLON = 12
WLAT = 6
WLEV = 2


def shifted(shard, axis, by):
    count = lax.axis_size(axis)
    return lax.ppermute(shard, axis, [(i, (i + by) % count) for i in range(count)])


def to_windows(grid):
    span_lon, span_lat, span_lev = (grid.shape[0], grid.shape[1], grid.shape[2])
    trailing = grid.shape[3:]
    blocks = grid.reshape(
        (span_lon // WLON, WLON, span_lat // WLAT, WLAT, span_lev // WLEV, WLEV) + trailing
    )
    axes_order = (0, 2, 4, 1, 3, 5) + tuple(range(6, 6 + len(trailing)))
    return blocks.transpose(axes_order).reshape((-1, WLON * WLAT * WLEV) + trailing)


def from_windows(windows, span_lon, span_lat, span_lev):
    width = windows.shape[-1]
    blocks = windows.reshape(
        span_lon // WLON, span_lat // WLAT, span_lev // WLEV, WLON, WLAT, WLEV, width
    )
    return blocks.transpose(0, 3, 1, 4, 2, 5, 6).reshape(span_lon, span_lat, span_lev, width)


def region_grid(lat_shifted, lat_total, levels):
    half_lat = WLAT // 2
    half_lev = WLEV // 2
    lat_orig = (lat_shifted + half_lat) % lat_total
    lat_region = jnp.where(
        lat_orig < half_lat, 2, jnp.where(lat_orig >= lat_total - (WLAT - half_lat), 1, 0)
    )
    lev_orig = (jnp.arange(levels, dtype=jnp.int32) + half_lev) % levels
    lev_region = jnp.where(
        lev_orig < half_lev, 2, jnp.where(lev_orig >= levels - (WLEV - half_lev), 1, 0)
    )
    return (lat_region[:, None] * 3 + lev_region[None, :]).astype(jnp.int32)


def window_terms(w_qkv, w_out, carry, inputs):
    win_tokens, win_cotan, win_region = inputs
    seq_len = win_tokens.shape[0]
    inner = H * E
    score_scale = 1.0 / math.sqrt(E)
    contract_rows = (((0,), (0,)), ((), ()))
    contract_cols = (((1,), (1,)), ((), ()))
    projected = jnp.dot(win_tokens, w_qkv, preferred_element_type=jnp.float32).astype(jnp.bfloat16)
    query_part = projected[:, :inner].reshape(seq_len, H, E)
    key_part = projected[:, inner : 2 * inner].reshape(seq_len, H, E)
    value_part = projected[:, 2 * inner :].reshape(seq_len, H, E)
    allowed = win_region[:, None] == win_region[None, :]
    scores = (
        jnp.einsum("shd,thd->hst", query_part, key_part, preferred_element_type=jnp.float32)
        * score_scale
    )
    scores = jnp.where(allowed[None], scores, -1e30)
    probs = jax.nn.softmax(scores, axis=-1)
    probs_b = probs.astype(jnp.bfloat16)
    attended = (
        jnp.einsum("hst,thd->shd", probs_b, value_part, preferred_element_type=jnp.float32)
        .astype(jnp.bfloat16)
        .reshape(seq_len, inner)
    )
    mixed = jnp.dot(attended, w_out, preferred_element_type=jnp.float32)
    centred = mixed - jnp.mean(mixed, axis=-1, keepdims=True)
    rstd_row = lax.rsqrt(jnp.mean(centred * centred, axis=-1, keepdims=True) + 1e-05)
    normed = centred * rstd_row
    upstream = win_cotan.astype(jnp.float32)
    d_mixed = rstd_row * (
        upstream
        - jnp.mean(upstream, axis=-1, keepdims=True)
        - normed * jnp.mean(upstream * normed, axis=-1, keepdims=True)
    )
    d_mixed = d_mixed.astype(jnp.bfloat16)
    out_term = lax.dot_general(attended, d_mixed, contract_rows, preferred_element_type=jnp.float32)
    d_attended = (
        lax.dot_general(d_mixed, w_out, contract_cols, preferred_element_type=jnp.float32)
        .astype(jnp.bfloat16)
        .reshape(seq_len, H, E)
    )
    d_probs = jnp.einsum("shd,thd->hst", d_attended, value_part, preferred_element_type=jnp.float32)
    d_values = jnp.einsum(
        "hst,shd->thd", probs_b, d_attended, preferred_element_type=jnp.float32
    ).astype(jnp.bfloat16)
    d_scores = (
        probs * (d_probs - jnp.sum(d_probs * probs, axis=-1, keepdims=True)) * score_scale
    ).astype(jnp.bfloat16)
    d_query = jnp.einsum(
        "hst,thd->shd", d_scores, key_part, preferred_element_type=jnp.float32
    ).astype(jnp.bfloat16)
    d_keys = jnp.einsum(
        "hst,shd->thd", d_scores, query_part, preferred_element_type=jnp.float32
    ).astype(jnp.bfloat16)
    d_projected = jnp.concatenate(
        [
            d_query.reshape(seq_len, inner),
            d_keys.reshape(seq_len, inner),
            d_values.reshape(seq_len, inner),
        ],
        axis=-1,
    )
    qkv_term = lax.dot_general(
        win_tokens, d_projected, contract_rows, preferred_element_type=jnp.float32
    )
    path_grad = lax.dot_general(
        d_projected, w_qkv, contract_cols, preferred_element_type=jnp.float32
    ).astype(jnp.bfloat16)
    return ((carry[0] + qkv_term, carry[1] + out_term), path_grad)


def body(tokens, cotangent, w_qkv, w_out):
    width_lon, width_lat, levels = (tokens.shape[0], tokens.shape[1], tokens.shape[2])
    half_lon, half_lat, half_lev = (WLON // 2, WLAT // 2, WLEV // 2)
    east_piece = shifted((tokens[:half_lon], cotangent[:half_lon]), "lon", -1)
    lon_tokens = jnp.concatenate([tokens[half_lon:], east_piece[0]], axis=0)
    lon_cotan = jnp.concatenate([cotangent[half_lon:], east_piece[1]], axis=0)
    north_piece = shifted((lon_tokens[:, :half_lat], lon_cotan[:, :half_lat]), "lat", -1)
    ext_tokens = jnp.concatenate([lon_tokens[:, half_lat:], north_piece[0]], axis=1)
    ext_cotan = jnp.concatenate([lon_cotan[:, half_lat:], north_piece[1]], axis=1)
    ext_tokens = jnp.roll(ext_tokens, -half_lev, axis=2)
    ext_cotan = jnp.roll(ext_cotan, -half_lev, axis=2)
    lat_total = width_lat * lax.axis_size("lat")
    lat_shifted = lax.axis_index("lat") * width_lat + jnp.arange(width_lat, dtype=jnp.int32)
    regions = region_grid(lat_shifted, lat_total, levels)
    regions = jnp.broadcast_to(regions[None], (width_lon, width_lat, levels))
    initial = (jnp.zeros((D, 3 * H * E), jnp.float32), jnp.zeros((H * E, D), jnp.float32))

    def step_fn(carry, inputs):
        return window_terms(w_qkv, w_out, carry, inputs)

    sums, path_windows = lax.scan(
        step_fn, initial, (to_windows(ext_tokens), to_windows(ext_cotan), to_windows(regions))
    )
    path_ext = from_windows(path_windows, width_lon, width_lat, levels)
    path_ext = jnp.roll(path_ext, half_lev, axis=2)
    from_south = shifted(path_ext[:, width_lat - half_lat :], "lat", 1)
    path_lon = jnp.concatenate([from_south, path_ext[:, : width_lat - half_lat]], axis=1)
    from_west = shifted(path_lon[width_lon - half_lon :], "lon", 1)
    path_own = jnp.concatenate([from_west, path_lon[: width_lon - half_lon]], axis=0)
    grad_tokens = (cotangent.astype(jnp.float32) + path_own.astype(jnp.float32)).astype(
        jnp.bfloat16
    )
    flat_qkv = sums[0].reshape(-1)
    flat_out = sums[1].reshape(-1)
    summed = (
        lax.psum_scatter(flat_qkv, ("lon", "lat"), scatter_dimension=0, tiled=True),
        lax.psum_scatter(flat_out, ("lon", "lat"), scatter_dimension=0, tiled=True),
    )
    token_count = width_lon * width_lat * levels * lax.axis_size("lon") * lax.axis_size("lat")
    norm_factor = 1.0 / math.sqrt(token_count)
    return (grad_tokens, summed[0] * norm_factor, summed[1] * norm_factor)


def solution(mesh):
    in_specs = (P("lon", "lat", None, None), P("lon", "lat", None, None), P(), P())
    out_specs = (P("lon", "lat", None, None), P(("lon", "lat")), P(("lon", "lat")))
    return jax.shard_map(body, mesh=mesh, in_specs=in_specs, out_specs=out_specs, check_vma=False)
```

profile of v0, /device:TPU:1, one launch (start us, length us, event | category | flops | bytes accessed | tf_op | source)
XLA Modules:
  0.0 527.3 jit_solution(6412373008270340872)
XLA Ops:
  8.3 9.9 %collective-permute-start.2 = (bf16[6,6,4,512]{3,2,1,0:T(4,128)(2,1)S(1)}, bf16[6,6,4,512]{3,2,1,0:T(4,128)(2,1)S(1)}, u32[]{:S(2)}, u32[]{:S(2)}) collective-permute-start(bf16[6,6,4,512]{3,2,1,0:T(4,128)(2,1)S(1)} %slice.74), channel_id=1, source_target_pairs={{0,504},{8,0},{16,8},{24,16},{32,24},{40,32},{48,40},{56,48},{64,5... | collective-permute-start | bytes 442376 | tf_op jit(solution)/shard_map/ppermute | solution.py:18
  19.2 3.0 collective-permute-start
  23.5 3.1 collective-permute-start.3
  27.7 8.9 %collective-permute-start.1 = (bf16[24,3,4,512]{3,2,1,0:T(4,128)(2,1)}, bf16[24,3,4,512]{3,2,1,0:T(4,128)(2,1)}, u32[]{:S(2)}, u32[]{:S(2)}) collective-permute-start(bf16[24,3,4,512]{3,2,1,0:T(4,128)(2,1)} %get-tuple-element.117), channel_id=1, source_target_pairs={{0,7},{1,0},{2,1},{3,2},{4,3},{5,4},{6,5},{7,6},{8,15},{9,8},{10,9... | collective-permute-start | bytes 884744 | tf_op jit(solution)/shard_map/ppermute | solution.py:18
  61.4 168.9 %while.15 = (s32[]{:T(128)}, f32[512,1536]{1,0:T(8,128)S(1)}, f32[512,512]{1,0:T(8,128)}, bf16[4,144,512]{2,1,0:T(8,128)(2,1)}, bf16[4,144,512]{2,1,0:T(8,128)(2...) while((s32[]{:T(128)}, f32[512,1536]{1,0:T(8,128)S(1)}, ...), condition=%wide.region_8.9_spmd.clone, body=%wide.region_0.8_spmd.clone.sunk | while | flops 1048102208 | bytes 49818332 | solution.py:144
  70.2 3.5 fusion.130
  80.0 3.0 convolution_convert_fusion.12
  87.5 5.3 %fusion.135 = bf16[16,32,144]{2,1,0:T(8,128)(2,1)} fusion(bf16[144,16,32]{0,2,1:T(8,128)(2,1)S(1)} %bitcast.155, f32[16,144,144]{1,2,0:T(8,128)} %fusion.133, f32[16,144,144]{1,2,0:T(8,128)} %get-tuple-element.185, f32[16,144]{1,0:T(8,128)S(1)} %get-tuple-element.186), kind=kOutput, calls=%fused_computation.15.clone.1 | convolution fusion | flops 23632272 | bytes 2958336 | tf_op jit(solution)/shard_map/while/body/eval_jaxpr/hst,thd->shd/dot_general | solution.py:101
  92.8 5.4 %fusion.134 = bf16[16,32,144]{2,1,0:T(8,128)(2,1)} fusion(bf16[144,16,32]{0,2,1:T(8,128)(2,1)} %bitcast.153, f32[16,144,144]{1,2,0:T(8,128)} %fusion.133, f32[16,144,144]{1,2,0:T(8,128)} %get-tuple-element.185, f32[16,144]{1,0:T(8,128)S(1)} %get-tuple-element.186), kind=kOutput, calls=%fused_computation.16.clone.1 | convolution fusion | flops 23632272 | bytes 2958336 | tf_op jit(solution)/shard_map/while/body/eval_jaxpr/hst,shd->thd/dot_general | solution.py:104
  112.4 3.5 fusion.130
  122.3 3.0 convolution_convert_fusion.12
  129.7 5.3 %fusion.135 = bf16[16,32,144]{2,1,0:T(8,128)(2,1)} fusion(bf16[144,16,32]{0,2,1:T(8,128)(2,1)S(1)} %bitcast.155, f32[16,144,144]{1,2,0:T(8,128)} %fusion.133, f32[16,144,144]{1,2,0:T(8,128)} %get-tuple-element.185, f32[16,144]{1,0:T(8,128)S(1)} %get-tuple-element.186), kind=kOutput, calls=%fused_computation.15.clone.1 | convolution fusion | flops 23632272 | bytes 2958336 | tf_op jit(solution)/shard_map/while/body/eval_jaxpr/hst,thd->shd/dot_general | solution.py:101
  135.0 5.4 %fusion.134 = bf16[16,32,144]{2,1,0:T(8,128)(2,1)} fusion(bf16[144,16,32]{0,2,1:T(8,128)(2,1)} %bitcast.153, f32[16,144,144]{1,2,0:T(8,128)} %fusion.133, f32[16,144,144]{1,2,0:T(8,128)} %get-tuple-element.185, f32[16,144]{1,0:T(8,128)S(1)} %get-tuple-element.186), kind=kOutput, calls=%fused_computation.16.clone.1 | convolution fusion | flops 23632272 | bytes 2958336 | tf_op jit(solution)/shard_map/while/body/eval_jaxpr/hst,shd->thd/dot_general | solution.py:104
  154.6 3.5 fusion.130
  164.5 3.0 convolution_convert_fusion.12
  172.0 5.3 %fusion.135 = bf16[16,32,144]{2,1,0:T(8,128)(2,1)} fusion(bf16[144,16,32]{0,2,1:T(8,128)(2,1)S(1)} %bitcast.155, f32[16,144,144]{1,2,0:T(8,128)} %fusion.133, f32[16,144,144]{1,2,0:T(8,128)} %get-tuple-element.185, f32[16,144]{1,0:T(8,128)S(1)} %get-tuple-element.186), kind=kOutput, calls=%fused_computation.15.clone.1 | convolution fusion | flops 23632272 | bytes 2958336 | tf_op jit(solution)/shard_map/while/body/eval_jaxpr/hst,thd->shd/dot_general | solution.py:101
  177.3 5.4 %fusion.134 = bf16[16,32,144]{2,1,0:T(8,128)(2,1)} fusion(bf16[144,16,32]{0,2,1:T(8,128)(2,1)} %bitcast.153, f32[16,144,144]{1,2,0:T(8,128)} %fusion.133, f32[16,144,144]{1,2,0:T(8,128)} %get-tuple-element.185, f32[16,144]{1,0:T(8,128)S(1)} %get-tuple-element.186), kind=kOutput, calls=%fused_computation.16.clone.1 | convolution fusion | flops 23632272 | bytes 2958336 | tf_op jit(solution)/shard_map/while/body/eval_jaxpr/hst,shd->thd/dot_general | solution.py:104
  196.9 3.5 fusion.130
  206.7 3.0 convolution_convert_fusion.12
  214.2 5.3 %fusion.135 = bf16[16,32,144]{2,1,0:T(8,128)(2,1)} fusion(bf16[144,16,32]{0,2,1:T(8,128)(2,1)S(1)} %bitcast.155, f32[16,144,144]{1,2,0:T(8,128)} %fusion.133, f32[16,144,144]{1,2,0:T(8,128)} %get-tuple-element.185, f32[16,144]{1,0:T(8,128)S(1)} %get-tuple-element.186), kind=kOutput, calls=%fused_computation.15.clone.1 | convolution fusion | flops 23632272 | bytes 2958336 | tf_op jit(solution)/shard_map/while/body/eval_jaxpr/hst,thd->shd/dot_general | solution.py:101
  219.5 5.4 %fusion.134 = bf16[16,32,144]{2,1,0:T(8,128)(2,1)} fusion(bf16[144,16,32]{0,2,1:T(8,128)(2,1)} %bitcast.153, f32[16,144,144]{1,2,0:T(8,128)} %fusion.133, f32[16,144,144]{1,2,0:T(8,128)} %get-tuple-element.185, f32[16,144]{1,0:T(8,128)S(1)} %get-tuple-element.186), kind=kOutput, calls=%fused_computation.16.clone.1 | convolution fusion | flops 23632272 | bytes 2958336 | tf_op jit(solution)/shard_map/while/body/eval_jaxpr/hst,shd->thd/dot_general | solution.py:104
  239.3 3.6 collective-permute-done.4
  245.4 10.1 %collective-permute-done.5 = bf16[6,6,4,512]{3,2,1,0:T(4,128)(2,1)S(1)} collective-permute-done((bf16[6,6,4,512]{3,2,1,0:T(4,128)(2,1)S(1)}, bf16[6,6,4,512]{3,2,1,0:T(4,128)(2,1)S(1)}, u32[]{:S(2)}, u32[]{:S(2)}) %collective-permute-start.5) | collective-permute-done | bytes 147488 | tf_op jit(solution)/shard_map/ppermute | solution.py:18
  256.8 260.9 %all-reduce.5.cloned.1.call-done = (f32[786432]{0:T(1024)}, f32[262144]{0:T(1024)}) async-done(((f32[786432]{0:T(1024)}, f32[262144]{0:T(1024)}), (f32[786432]{0:T(1024)}, f32[262144]{0:T(1024)})) %all-reduce.5.cloned.1.call-update) | async-done | bytes 4194320
  (261 shorter events, 144.3 us)
Async XLA Ops:
  7.2 15.1 %slice-start = ((bf16[24,6,4,512]{3,2,1,0:T(4,128)(2,1)}), bf16[18,6,4,512]{3,2,1,0:T(4,128)(2,1)S(1)}, s32[]{:S(2)}) async-start(bf16[24,6,4,512]{3,2,1,0:T(4,128)(2,1)} %param.7), calls=%async_computation.1 | async-start | bytes 884736 | tf_op jit(solution)/shard_map/slice | solution.py:129
  7.2 19.5 %slice-start.1 = ((bf16[24,6,4,512]{3,2,1,0:T(4,128)(2,1)}), bf16[18,6,4,512]{3,2,1,0:T(4,128)(2,1)S(1)}, s32[]{:S(2)}) async-start(bf16[24,6,4,512]{3,2,1,0:T(4,128)(2,1)} %param.6), calls=%async_computation.2 | async-start | bytes 884736 | tf_op jit(solution)/shard_map/slice | solution.py:128
  7.2 510.6 %all-reduce.5.cloned.1.call-start = ((), (), s32[]{:S(2)}) async-start(), calls=%async_computation | async-start | bytes 8388608
  8.3 14.0 %collective-permute-start.2 = (bf16[6,6,4,512]{3,2,1,0:T(4,128)(2,1)S(1)}, bf16[6,6,4,512]{3,2,1,0:T(4,128)(2,1)S(1)}, u32[]{:S(2)}, u32[]{:S(2)}) collective-permute-start(bf16[6,6,4,512]{3,2,1,0:T(4,128)(2,1)S(1)} %slice.74), channel_id=1, source_target_pairs={{0,504},{8,0},{16,8},{24,16},{32,24},{40,32},{48,40},{56,48},{64,5... | collective-permute-start | bytes 442376 | tf_op jit(solution)/shard_map/ppermute | solution.py:18
  19.2 7.4 %collective-permute-start = (bf16[6,6,4,512]{3,2,1,0:T(4,128)(2,1)S(1)}, bf16[6,6,4,512]{3,2,1,0:T(4,128)(2,1)S(1)}, u32[]{:S(2)}, u32[]{:S(2)}) collective-permute-start(bf16[6,6,4,512]{3,2,1,0:T(4,128)(2,1)S(1)} %slice.68), channel_id=1, source_target_pairs={{0,504},{8,0},{16,8},{24,16},{32,24},{40,32},{48,40},{56,48},{64,5... | collective-permute-start | bytes 442376 | tf_op jit(solution)/shard_map/ppermute | solution.py:18
  23.5 14.9 %collective-permute-start.3 = (bf16[24,3,4,512]{3,2,1,0:T(4,128)(2,1)}, bf16[24,3,4,512]{3,2,1,0:T(4,128)(2,1)}, u32[]{:S(2)}, u32[]{:S(2)}) collective-permute-start(bf16[24,3,4,512]{3,2,1,0:T(4,128)(2,1)} %get-tuple-element.115), channel_id=1, source_target_pairs={{0,7},{1,0},{2,1},{3,2},{4,3},{5,4},{6,5},{7,6},{8,15},{9,8},{10,9... | collective-permute-start | bytes 884744 | tf_op jit(solution)/shard_map/ppermute | solution.py:18
  27.7 22.3 %collective-permute-start.1 = (bf16[24,3,4,512]{3,2,1,0:T(4,128)(2,1)}, bf16[24,3,4,512]{3,2,1,0:T(4,128)(2,1)}, u32[]{:S(2)}, u32[]{:S(2)}) collective-permute-start(bf16[24,3,4,512]{3,2,1,0:T(4,128)(2,1)} %get-tuple-element.117), channel_id=1, source_target_pairs={{0,7},{1,0},{2,1},{3,2},{4,3},{5,4},{6,5},{7,6},{8,15},{9,8},{10,9... | collective-permute-start | bytes 884744 | tf_op jit(solution)/shard_map/ppermute | solution.py:18
  67.5 6.2 %copy-start.5 = (bf16[144,512]{0,1:T(8,128)(2,1)}, bf16[144,512]{0,1:T(8,128)(2,1)S(1)}, u32[]{:S(2)}) copy-start(bf16[144,512]{0,1:T(8,128)(2,1)S(1)} %copy.59) | copy-start | bytes 442372 | tf_op jit(solution)/shard_map/while
  73.6 3.4 copy-start.15
  73.6 3.4 copy-start.8
  92.8 5.4 %copy-start.9 = (bf16[16,32,144]{2,1,0:T(8,128)(2,1)S(1)}, bf16[16,32,144]{2,1,0:T(8,128)(2,1)}, u32[]{:S(2)}) copy-start(bf16[16,32,144]{2,1,0:T(8,128)(2,1)} %convolution_convert_fusion.12) | copy-start | bytes 442372 | tf_op jit(solution)/shard_map/while
  109.7 6.2 %copy-start.5 = (bf16[144,512]{0,1:T(8,128)(2,1)}, bf16[144,512]{0,1:T(8,128)(2,1)S(1)}, u32[]{:S(2)}) copy-start(bf16[144,512]{0,1:T(8,128)(2,1)S(1)} %copy.59) | copy-start | bytes 442372 | tf_op jit(solution)/shard_map/while
  115.9 3.4 copy-start.15
  115.9 3.4 copy-start.8
  135.0 5.4 %copy-start.9 = (bf16[16,32,144]{2,1,0:T(8,128)(2,1)S(1)}, bf16[16,32,144]{2,1,0:T(8,128)(2,1)}, u32[]{:S(2)}) copy-start(bf16[16,32,144]{2,1,0:T(8,128)(2,1)} %convolution_convert_fusion.12) | copy-start | bytes 442372 | tf_op jit(solution)/shard_map/while
  151.9 6.2 %copy-start.5 = (bf16[144,512]{0,1:T(8,128)(2,1)}, bf16[144,512]{0,1:T(8,128)(2,1)S(1)}, u32[]{:S(2)}) copy-start(bf16[144,512]{0,1:T(8,128)(2,1)S(1)} %copy.59) | copy-start | bytes 442372 | tf_op jit(solution)/shard_map/while
  158.1 3.4 copy-start.8
  177.3 5.4 %copy-start.9 = (bf16[16,32,144]{2,1,0:T(8,128)(2,1)S(1)}, bf16[16,32,144]{2,1,0:T(8,128)(2,1)}, u32[]{:S(2)}) copy-start(bf16[16,32,144]{2,1,0:T(8,128)(2,1)} %convolution_convert_fusion.12) | copy-start | bytes 442372 | tf_op jit(solution)/shard_map/while
  194.2 6.2 %copy-start.5 = (bf16[144,512]{0,1:T(8,128)(2,1)}, bf16[144,512]{0,1:T(8,128)(2,1)S(1)}, u32[]{:S(2)}) copy-start(bf16[144,512]{0,1:T(8,128)(2,1)S(1)} %copy.59) | copy-start | bytes 442372 | tf_op jit(solution)/shard_map/while
  200.4 3.4 copy-start.8
  219.5 5.4 %copy-start.9 = (bf16[16,32,144]{2,1,0:T(8,128)(2,1)S(1)}, bf16[16,32,144]{2,1,0:T(8,128)(2,1)}, u32[]{:S(2)}) copy-start(bf16[16,32,144]{2,1,0:T(8,128)(2,1)} %convolution_convert_fusion.12) | copy-start | bytes 442372 | tf_op jit(solution)/shard_map/while
  236.4 19.0 %copy-start.13 = (bf16[24,6,4,512]{3,2,1,0:T(4,128)(2,1)S(1)}, bf16[24,6,4,512]{3,2,1,0:T(4,128)(2,1)}, u32[]{:S(2)}) copy-start(bf16[24,6,4,512]{3,2,1,0:T(4,128)(2,1)} %param.7) | copy-start | bytes 1769476
  237.3 5.6 %collective-permute-start.4 = (bf16[24,3,4,512]{3,2,1,0:T(4,128)(2,1)S(1)}, bf16[24,3,4,512]{3,2,1,0:T(4,128)(2,1)S(1)}, u32[]{:S(2)}, u32[]{:S(2)}) collective-permute-start(bf16[24,3,4,512]{3,2,1,0:T(4,128)(2,1)S(1)} %fusion.54), channel_id=1, source_target_pairs={{0,1},{1,2},{2,3},{3,4},{4,5},{5,6},{6,7},{7,0},{8,9},{9,10},{10,1... | collective-permute-start | bytes 884744 | tf_op jit(solution)/shard_map/ppermute | solution.py:18
  243.0 12.4 %collective-permute-start.5 = (bf16[6,6,4,512]{3,2,1,0:T(4,128)(2,1)S(1)}, bf16[6,6,4,512]{3,2,1,0:T(4,128)(2,1)S(1)}, u32[]{:S(2)}, u32[]{:S(2)}) collective-permute-start(bf16[6,6,4,512]{3,2,1,0:T(4,128)(2,1)S(1)} %pad_maximum_fusion.9), channel_id=1, source_target_pairs={{0,8},{8,16},{16,24},{24,32},{32,40},{40,48},{48,56},{56,64},{64,7... | collective-permute-start | bytes 442376 | tf_op jit(solution)/shard_map/ppermute | solution.py:18
  (51 other events, 121.1 us)
Sparse Core Ops, SparseCore 0:
  234.9 282.8 all-reduce.4
where the time goes:
time: 530 us; the launch traced here: 527 us
  waiting for transfers between devices  275 us (52%)
  matrix products  125 us (24%)
  local copies, waits for them, and re-layouts  57.4 us (11%)
  starting transfers between devices  29.2 us (6%)
  other arithmetic  25.8 us (5%)
  between operations  14.2 us (3%)
    unnamed x2, waiting for transfers between devices  261 us
    ppermute x6, starting transfers between devices, shifted(): lax.ppermute(shard, axis, [(i, (i + by) % count) for i in range(count)])  29.2 us
    dot_general x4, matrix products, window_terms(): jnp.einsum('hst,shd->thd', d_scores, query_part, preferred_element_type=j...  21.4 us
    dot_general x4, matrix products, window_terms(): jnp.einsum('hst,thd->shd', d_scores, key_part, preferred_element_type=jnp...  21.2 us
    sub x4, matrix products, window_terms(): probs = jax.nn.softmax(scores, axis=-1)  13.8 us
    ppermute x6, waiting for transfers between devices, shifted(): lax.ppermute(shard, axis, [(i, (i + by) % count) for i in range(count)])  13.8 us
    dot_general x4, matrix products, window_terms(): jnp.einsum('hst,shd->thd', probs_b, d_attended, preferred_element_type=jn...  12.1 us
    dot_general x4, matrix products, window_terms(): lax.dot_general(d_projected, w_qkv, contract_cols, preferred_element_type...  11.9 us
  transfers between devices with their start and end apart: 7, of which 3 were waited for; matrix products, arithmetic and copies ran while one was open for 4% of the time, Pallas kernels for 0%

commit v1 on v0

v1 whole, which is shorter than its diff:
```python
import functools
import math

import jax
import jax.numpy as jnp
from jax import lax
from jax.experimental import pallas as pl
from jax.experimental.pallas import tpu as pltpu
from jax.sharding import PartitionSpec as P

D = 512
H = 16
E = 32
WIN = 144
SLAB = 2 * WIN
TOK = 2 * SLAB
GROUP = 8
LANES = GROUP * WIN
SCALE = 1.0 / math.sqrt(E)
BF = jnp.bfloat16
F32 = jnp.float32
MESH = pl.DeviceIdType.MESH
NN = (((1,), (0,)), ((), ()))
NT = (((1,), (1,)), ((), ()))
TN = (((0,), (0,)), ((), ()))


def mm(a, b, dims=NN):
    return lax.dot_general(a, b, dims, preferred_element_type=F32)


def near(lon, lat):
    n_lon, n_lat = lax.axis_size("lon"), lax.axis_size("lat")
    return ((lax.axis_index("lon") + lon + n_lon) % n_lon, (lax.axis_index("lat") + lat + n_lat) % n_lat)


HALO = ((0, 1), (0, -1), (1, 0), (-1, 0), (1, -1), (-1, 1))


def halo_kernel(tok, cot, ext_tok, ext_cot, send, recv, local):
    barrier = pltpu.get_barrier_semaphore()
    for step in HALO:
        pl.semaphore_signal(barrier, inc=1, device_id=near(*step), device_id_type=MESH)
    pl.semaphore_wait(barrier, len(HALO))
    copies = []
    for a, (src, ext) in enumerate(((tok, ext_tok), (cot, ext_cot))):
        sends = (
            (src.at[6:18, 0:3], ext.at[0, :, 3:6], (0, -1)),
            (src.at[18:24, 3:6], ext.at[1, 0:6, 0:3], (0, 1)),
            (src.at[0:6, 3:6], ext.at[1, 6:12, 0:3], (-1, 1)),
            (src.at[0:6, 0:3], ext.at[1, 6:12, 3:6], (-1, 0)),
        )
        for k, (here, there, step) in enumerate(sends):
            copies.append(
                pltpu.make_async_remote_copy(
                    src_ref=here,
                    dst_ref=there,
                    send_sem=send.at[a, k],
                    recv_sem=recv.at[a, k],
                    device_id=near(*step),
                    device_id_type=MESH,
                )
            )
        copies.append(pltpu.make_async_copy(src.at[6:18, 3:6], ext.at[0, :, 0:3], local.at[a, 0]))
        copies.append(pltpu.make_async_copy(src.at[18:24, 0:3], ext.at[1, 0:6, 3:6], local.at[a, 1]))
    for copy in copies:
        copy.start()
    for copy in copies:
        copy.wait()


def halo(tok, cot):
    any_ = pl.BlockSpec(memory_space=pl.ANY)
    ext = jax.ShapeDtypeStruct((2, 12, 6, 4, D), BF)
    return pl.pallas_call(
        halo_kernel,
        out_shape=(ext, ext),
        in_specs=[any_] * 2,
        out_specs=(any_,) * 2,
        scratch_shapes=[
            pltpu.SemaphoreType.DMA((2, 4)),
            pltpu.SemaphoreType.DMA((2, 4)),
            pltpu.SemaphoreType.DMA((2, 2)),
        ],
        compiler_params=pltpu.CompilerParams(collective_id=0, has_side_effects=True),
        name="halo",
    )(tok, cot)


def lane_head():
    return lax.broadcasted_iota(jnp.int32, (WIN, 256), 1) // E


def stack_heads(x):
    lane = lane_head()
    zero = jnp.zeros_like(x)
    return jnp.concatenate([jnp.where(lane == h, x, zero) for h in range(GROUP)], axis=0)


def pick_heads(r):
    lane = lane_head()
    out = r[0:WIN]
    for h in range(1, GROUP):
        out = jnp.where(lane == h, r[h * WIN : (h + 1) * WIN], out)
    return out


def level_order(rows, natural):
    return natural == 4 * (rows % 72) + (rows // 72 + 1) % 4


def owner_order(i, p):
    x = 2 * ((p // 16) % 2) + (p // 128) % 2
    y = 2 * ((p // 4) % 4) + (p // 64) % 2
    return i == x * 128 + ((p // 32) % 2) * 64 + y * 8 + (p % 4) * 2 + p // 256


def one_hot(relation, shape, swap=False):
    a = lax.broadcasted_iota(jnp.int32, shape, 1 if swap else 0)
    b = lax.broadcasted_iota(jnp.int32, shape, 0 if swap else 1)
    return jnp.where(relation(a, b), 1.0, 0.0).astype(BF)


def region(pos, split_level, split_lat):
    return (pos // 72) * split_level + 2 * split_lat * ((pos % 6) // 3)


def window_kernel(tok, cot, wqkv, wout, path, grad, X, C, PR, A, DM, DA, DP, PT):
    lat = lax.axis_index("lat")
    last = lax.axis_size("lat") - 1
    order = one_hot(level_order, (SLAB, SLAB))
    for w in range(2):
        rows = pl.ds(w * SLAB, SLAB)
        X[rows, :] = mm(order, tok[w].reshape(SLAB, D)).astype(BF)
        C[rows, :] = mm(order, cot[w].reshape(SLAB, D)).astype(BF)
    for c in range(3):
        cols = pl.ds(c * D, D)
        PR[:, cols] = mm(X[...], wqkv[:, cols]).astype(BF)

    def parts(rows, g):
        return [PR[rows, c * D + g * 256 : c * D + (g + 1) * 256] for c in range(3)]

    def forward(i, _):
        rows = pl.ds(pl.multiple_of(i * WIN, WIN), WIN)
        split_lat = jnp.where(lat == jnp.where(i < 2, last, 0), 1, 0)
        key_region = region(lax.broadcasted_iota(jnp.int32, (WIN, 128), 0), i % 2, split_lat)
        for g in range(2):
            q, k, v = parts(rows, g)
            scores = mm(k, stack_heads(q), NT)
            probs_b = []
            for c in range(LANES // 128):
                cols = slice(c * 128, (c + 1) * 128)
                pos = lax.broadcasted_iota(jnp.int32, (1, 128), 1) + c * 128
                allowed = key_region == region(pos % WIN, i % 2, split_lat)
                s = jnp.where(allowed, scores[:, cols] * SCALE, -1e30)
                e = jnp.exp(s - jnp.max(s, axis=0, keepdims=True))
                p = e * (1.0 / jnp.sum(e, axis=0, keepdims=True))
                PT[i * 2 + g, :, cols] = p
                probs_b.append(p.astype(BF))
            probs_b = jnp.concatenate(probs_b, axis=1)
            A[rows, g * 256 : (g + 1) * 256] = pick_heads(mm(probs_b, v, TN)).astype(BF)
        return 0

    lax.fori_loop(0, 4, forward, 0)

    for i in range(4):
        rows = pl.ds(i * WIN, WIN)
        mixed = mm(A[rows, :], wout[...])
        centred = mixed - jnp.mean(mixed, axis=-1, keepdims=True)
        rstd = lax.rsqrt(jnp.mean(centred * centred, axis=-1, keepdims=True) + 1e-5)
        normed = centred * rstd
        up = C[rows, :].astype(F32)
        d_mixed = rstd * (
            up - jnp.mean(up, axis=-1, keepdims=True) - normed * jnp.mean(up * normed, axis=-1, keepdims=True)
        )
        d_mixed = d_mixed.astype(BF)
        DM[rows, :] = d_mixed
        DA[rows, :] = mm(d_mixed, wout[...], NT).astype(BF)

    owner = one_hot(owner_order, (D, D))
    grad[:, :, 3 * D :] = mm(mm(A[...], owner).astype(BF), DM[...], TN).reshape(16, 32, D)

    def backward(i, _):
        rows = pl.ds(pl.multiple_of(i * WIN, WIN), WIN)
        for g in range(2):
            q, k, v = parts(rows, g)
            d_att = stack_heads(DA[rows, g * 256 : (g + 1) * 256])
            d_probs = mm(v, d_att, NT)
            probs_b, d_scores = [], []
            for c in range(LANES // 128):
                cols = slice(c * 128, (c + 1) * 128)
                p = PT[i * 2 + g, :, cols]
                dp = d_probs[:, cols]
                probs_b.append(p.astype(BF))
                d_scores.append((p * (dp - jnp.sum(dp * p, axis=0, keepdims=True)) * SCALE).astype(BF))
            probs_b = jnp.concatenate(probs_b, axis=1)
            d_scores = jnp.concatenate(d_scores, axis=1)
            d_parts = (pick_heads(mm(d_scores, k, TN)), mm(d_scores, stack_heads(q)), mm(probs_b, d_att))
            for c, part in enumerate(d_parts):
                DP[rows, c * D + g * 256 : c * D + (g + 1) * 256] = part.astype(BF)
        return 0

    lax.fori_loop(0, 4, backward, 0)

    X[...] = mm(X[...], owner).astype(BF)
    for c in range(3):
        cols = pl.ds(c * D, D)
        grad[:, :, cols] = mm(X[...], DP[:, cols], TN).reshape(16, 32, D)
    back = one_hot(level_order, (SLAB, SLAB), swap=True)
    for w in range(2):
        grads = mm(DP[pl.ds(w * SLAB, SLAB), :], wqkv[...], NT).astype(BF)
        path[w] = mm(back, grads).astype(BF).reshape(path.shape[1:])


def windows(ext_tok, ext_cot, wqkv, wout):
    vm = pl.BlockSpec(memory_space=pltpu.VMEM)
    rows = pltpu.VMEM((TOK, D), BF)
    wide = pltpu.VMEM((TOK, 3 * D), BF)
    return pl.pallas_call(
        window_kernel,
        out_shape=(jax.ShapeDtypeStruct(ext_tok.shape, BF), jax.ShapeDtypeStruct((16, 32, 4 * D), F32)),
        in_specs=[vm] * 4,
        out_specs=(vm,) * 2,
        scratch_shapes=[rows, rows, wide, rows, rows, rows, wide, pltpu.VMEM((8, WIN, LANES), F32)],
        compiler_params=pltpu.CompilerParams(vmem_limit_bytes=56 * 2**20),
        name="windows",
    )(ext_tok, ext_cot, wqkv, wout)


ROUTES = (
    ("y", "z", "x", 1, 0, 3),
    ("z", "x", "y", 1, 3, 6),
    ("x", "y", "z", 1, 6, 8),
    ("y", "z", "x", -1, 8, 11),
    ("z", "x", "y", -1, 11, 14),
    ("x", "y", "z", -1, 14, 16),
)
SIZES = {"x": 4, "y": 8, "z": 8}
FAR = tuple((a, b, c) for a in (1, 0) for b in (2, 1, 3, 0) for c in (2, 1, 3, 0) if a + b + c)


def position():
    lon, lat = lax.axis_index("lon"), lax.axis_index("lat")
    return {"x": lon // 16, "y": lon % 8, "z": (lat // 2) * 2 + (lon // 8) % 2, "core": lat % 2}


def device(at):
    return (at["x"] * 16 + (at["z"] % 2) * 8 + at["y"], (at["z"] // 2) * 2 + at["core"])


def moved(at, **steps):
    new = dict(at)
    for axis, step in steps.items():
        size = SIZES.get(axis, 2)
        new[axis] = (at[axis] + step + size) % size
    return device(new)


def sum_kernel(path, grad, own_path, total, R0, T, R1, R2, R3, F, Q, s0, r0, s, r, sf, rf, sh, rh, lh):
    at = position()
    bit = {axis: at[axis] % 2 for axis in SIZES}
    core = at["core"]
    others = [near(*step) for step in HALO]
    others += [moved(at, core=1)]
    others += [moved(at, **{axis: step}) for axis in SIZES for step in (1, -1)]
    others += [moved(at, x=2 * a, y=2 * b, z=2 * c) for a, b, c in FAR]
    barrier = pltpu.get_barrier_semaphore()
    for other in others:
        pl.semaphore_signal(barrier, inc=1, device_id=other, device_id_type=MESH)
    pl.semaphore_wait(barrier, len(others))

    def remote(src, dst, send, recv, to):
        copy = pltpu.make_async_remote_copy(
            src_ref=src, dst_ref=dst, send_sem=send, recv_sem=recv, device_id=to, device_id_type=MESH
        )
        copy.start()
        return copy

    first = []
    for n, (_, _, _, _, lo, hi) in enumerate(ROUTES):
        cols = pl.ds(lo * 128, (hi - lo) * 128)
        first.append(
            remote(grad.at[1 - core, :, :, :, :, cols], R0.at[:, :, :, :, cols], s0.at[n], r0.at[n], moved(at, core=1))
        )

    backs = [
        remote(path.at[0, :, 3:6], own_path.at[6:18, 0:3], sh.at[0], rh.at[0], near(0, 1)),
        remote(path.at[1, 0:6, 0:3], own_path.at[18:24, 3:6], sh.at[1], rh.at[1], near(0, -1)),
        remote(path.at[1, 6:12, 0:3], own_path.at[0:6, 3:6], sh.at[2], rh.at[2], near(1, -1)),
        remote(path.at[1, 6:12, 3:6], own_path.at[0:6, 0:3], sh.at[3], rh.at[3], near(1, 0)),
    ]
    locals_ = [
        pltpu.make_async_copy(path.at[0, :, 0:3], own_path.at[6:18, 3:6], lh.at[0]),
        pltpu.make_async_copy(path.at[1, 0:6, 3:6], own_path.at[18:24, 0:3], lh.at[1]),
    ]
    for copy in locals_:
        copy.start()

    def pick(fixed, cols):
        dims = [pl.ds(fixed[axis], 1) if axis in fixed else slice(None) for axis in ("x", "y", "z")]
        return (*dims, slice(None), cols)

    sent = []
    done = [{} for _ in ROUTES]
    flying = list(first)
    for stage in range(4):
        into = (R0, R1, R2, R3)[stage]
        for n, route in enumerate(ROUTES):
            sense, lo, hi = route[3:]
            cols = pl.ds(lo * 128, (hi - lo) * 128)
            flying[n].wait_recv()
            sent.append(flying[n])
            held = pick(done[n], cols)
            if stage == 0:
                T[held] = grad[core, :, :, :, :, cols] + R0[held]
            elif stage < 3:
                T[held] = T[held] + into[held]
            else:
                for c in range(lo, hi):
                    held = pick(done[n], pl.ds(c * 128, 128))
                    F[pl.ds(c, 32, stride=16), :] = (T[held] + into[held]).reshape(32, 128)
            if stage < 3:
                axis = route[stage]
                go = pick({**done[n], axis: 1 - bit[axis]}, cols)
                done[n][axis] = bit[axis]
                flying[n] = remote(
                    T.at[go],
                    (R1, R2, R3)[stage].at[go],
                    s.at[stage, n],
                    r.at[stage, n],
                    moved(at, **{axis: sense * (1 - 2 * bit[axis])}),
                )

    def row(a, b, c):
        place = ((at["x"] // 2 + a) % 2) * 16 + ((at["y"] // 2 + b) % 4) * 4 + (at["z"] // 2 + c) % 4
        return pl.ds(pl.multiple_of(place * 16, 16), 16)

    last = []
    for n, (a, b, c) in enumerate(FAR):
        last.append(
            remote(F.at[row(a, b, c)], Q.at[n], sf.at[n], rf.at[n], moved(at, x=2 * a, y=2 * b, z=2 * c))
        )
    value = F[row(0, 0, 0), :]
    for n, copy in enumerate(last):
        copy.wait_recv()
        value = value + Q[n]
    total[...] = value
    for copy in sent + last:
        copy.wait_send()
    for copy in backs + locals_:
        copy.wait()


def sums(path, grad):
    vm = pl.BlockSpec(memory_space=pltpu.VMEM)
    half = pltpu.VMEM((2, 2, 2, 32, 4 * D), F32)
    dma = pltpu.SemaphoreType.DMA
    n = len(ROUTES)
    return pl.pallas_call(
        sum_kernel,
        out_shape=(jax.ShapeDtypeStruct((24, 6, 4, D), BF), jax.ShapeDtypeStruct((16, 128), F32)),
        in_specs=[vm] * 2,
        out_specs=(vm,) * 2,
        scratch_shapes=[
            *(half,) * 5,
            pltpu.VMEM((32 * 16, 128), F32),
            pltpu.VMEM((len(FAR), 16, 128), F32),
            dma((n,)),
            dma((n,)),
            dma((3, n)),
            dma((3, n)),
            dma((len(FAR),)),
            dma((len(FAR),)),
            dma((4,)),
            dma((4,)),
            dma((2,)),
        ],
        compiler_params=pltpu.CompilerParams(
            collective_id=1, has_side_effects=True, vmem_limit_bytes=56 * 2**20
        ),
        name="sums",
    )(path, grad.reshape(2, 2, 2, 2, 32, 4 * D))


def body(tokens, cotangent, w_qkv, w_out):
    ext_tok, ext_cot = halo(tokens, cotangent)
    path, grad = windows(ext_tok, ext_cot, w_qkv, w_out)
    own_path, total = sums(path, grad)
    grad_tokens = (cotangent.astype(F32) + own_path.astype(F32)).astype(BF)
    count = tokens.shape[0] * tokens.shape[1] * tokens.shape[2] * lax.axis_size("lon") * lax.axis_size("lat")
    total = total.reshape(-1) * (1.0 / math.sqrt(count))
    return grad_tokens, total[: 3 * D], total[3 * D :]


def solution(mesh):
    in_specs = (P("lon", "lat", None, None), P("lon", "lat", None, None), P(), P())
    out_specs = (P("lon", "lat", None, None), P(("lon", "lat")), P(("lon", "lat")))
    return jax.shard_map(body, mesh=mesh, in_specs=in_specs, out_specs=out_specs, check_vma=False)
```

time: 530 us -> 94.2 us (0.18)
  waiting for transfers between devices: 275 us -> 0 us
  matrix products: 125 us -> 0 us
  Pallas kernels: 0 us -> 89.4 us
  local copies, waits for them, and re-layouts: 57.4 us -> 1.19 us
  starting transfers between devices: 29.2 us -> 0 us
  other arithmetic: 25.8 us -> 2.19 us
  between operations: 14.2 us -> 0.66 us
    unnamed x2 -> x0, waiting for transfers between devices: 261 us -> none
    dot_general x44 -> x0, matrix products: 111 us -> none  [the longest x4 21.4 us: window_terms(): jnp.einsum('hst,shd->thd', d_scores, query_part, preferred_element_type=j...]
    pallas_call x0 -> x3, Pallas kernels: none -> 89.4 us  [the longest x1 39.8 us: sums(): pl.pallas_call(sum_kernel, out_shape=(jax.ShapeDtypeStruct((24, 6, 4, D),...]
    ppermute x6 -> x0, starting transfers between devices: 29.2 us -> none  [shifted(): lax.ppermute(shard, axis, [(i, (i + by) % count) for i in range(count)])]
    slice x23 -> x2, local copies, waits for them, and re-layouts: 20.3 us -> 1.18 us  [body(): return (grad_tokens, total[:3 * D], total[3 * D:])]
    reshape x11 -> x0, local copies, waits for them, and re-layouts: 18.8 us -> none  [the longest x4 9.7 us: to_windows(): grid.reshape((span_lon // WLON, WLON, span_lat // WLAT, WLAT, span_lev //...]
    sub x4 -> x0, matrix products: 13.8 us -> none  [window_terms(): probs = jax.nn.softmax(scores, axis=-1)]
    ppermute x6 -> x0, waiting for transfers between devices: 13.8 us -> none  [shifted(): lax.ppermute(shard, axis, [(i, (i + by) % count) for i in range(count)])]
  transfers between devices with their start and end apart: 7 -> 0, of which waited for: 3 -> 0; matrix products, arithmetic and copies ran while one was open for 4% -> 0% of each run, Pallas kernels for 0% -> 0%
where the time goes in v1:
time: 94.2 us; the launch traced here: 93.5 us
  Pallas kernels  89.4 us (95%)
  other arithmetic  2.19 us (2%)
  local copies, waits for them, and re-layouts  1.19 us (1%)
    pallas_call x1, Pallas kernels, sums(): pl.pallas_call(sum_kernel, out_shape=(jax.ShapeDtypeStruct((24, 6, 4, D),...  39.8 us
    pallas_call x1, Pallas kernels, halo(): pl.pallas_call(halo_kernel, out_shape=(ext, ext), in_specs=[any_] * 2, ou...  27.6 us
    pallas_call x1, Pallas kernels, windows(): pl.pallas_call(window_kernel, out_shape=(jax.ShapeDtypeStruct(ext_tok.sha...  22 us
    convert_element_type x1, other arithmetic, body(): grad_tokens = (cotangent.astype(F32) + own_path.astype(F32)).astype(BF)  2.19 us

profile of v1, /device:TPU:1, one launch (start us, length us, event | category | flops | bytes accessed | tf_op | source)
XLA Modules:
  0.0 93.5 jit_solution(8920099773864933031)
XLA Ops:
  0.6 27.6 %halo.1 = (bf16[2,12,6,4,512]{4,3,2,1,0:T(4,128)(2,1)}, bf16[2,12,6,4,512]{4,3,2,1,0:T(4,128)(2,1)}) custom-call(bf16[24,6,4,512]{3,2,1,0:T(4,128)(2,1)} %tok.1, bf16[24,6,4,512]{3,2,1,0:T(4,128)(2,1)} %cot.1), custom_call_target="tpu_custom_call" | custom-call | tf_op jit(solution)/shard_map/halo/pallas_call | solution.py:75
  28.3 22.0 %windows.1 = (bf16[2,12,6,4,512]{4,3,2,1,0:T(4,128)(2,1)}, f32[16,32,2048]{2,1,0:T(8,128)}) custom-call(bf16[2,12,6,4,512]{4,3,2,1,0:T(4,128)(2,1)} %get-tuple-element.9.tok, bf16[2,12,6,4,512]{4,3,2,1,0:T(4,128)(2,1)} %get-tuple-element.10.cot, bf16[512,1536]{1,0:T(8,128)(2,1)} %wqkv.1, bf16[512,512]{1,0:T(8,128)(2,1)} %wout.1), custom_call_target="tpu_custom_call" | custom-call | tf_op jit(solution)/shard_map/windows/pallas_call | solution.py:219
  50.2 0.0 copy-start
  50.2 39.8 %sums.1 = (bf16[24,6,4,512]{3,2,1,0:T(4,128)(2,1)}, f32[16,128]{1,0:T(8,128)}) custom-call(bf16[2,12,6,4,512]{4,3,2,1,0:T(4,128)(2,1)} %get-tuple-element.11.path, f32[2,2,2,2,32,2048]{5,4,3,2,1,0:T(8,128)} %bitcast.5), custom_call_target="tpu_custom_call" | custom-call | tf_op jit(solution)/shard_map/sums/pallas_call | solution.py:359
  90.1 0.0 copy-start.1
  90.1 0.0 copy-done
  90.1 2.2 %add_convert_fusion = bf16[24,6,4,512]{3,2,1,0:T(4,128)(2,1)} fusion(bf16[24,6,4,512]{3,2,1,0:T(4,128)(2,1)} %get-tuple-element.13, bf16[24,6,4,512]{3,2,1,0:T(4,128)(2,1)S(1)} %copy-done), kind=kLoop, calls=%fused_computation | loop fusion | flops 1179648 | bytes 1769472 | tf_op jit(solution)/shard_map/convert_element_type | solution.py:389
  92.3 0.0 copy-done.1
  92.3 0.6 slice_bitcast_fusion.1
  92.9 0.6 slice_bitcast_fusion
  (1 shorter events, 0.0 us)
Async XLA Ops:
  50.2 39.9 %copy-start = (bf16[24,6,4,512]{3,2,1,0:T(4,128)(2,1)S(1)}, bf16[24,6,4,512]{3,2,1,0:T(4,128)(2,1)}, u32[]{:S(2)}) copy-start(bf16[24,6,4,512]{3,2,1,0:T(4,128)(2,1)} %cot.1) | copy-start | bytes 1769476
  90.1 2.2 %copy-start.1 = (f32[16,128]{1,0:T(8,128)S(1)}, f32[16,128]{1,0:T(8,128)}, u32[]{:S(2)}) copy-start(f32[16,128]{1,0:T(8,128)} %get-tuple-element.14) | copy-start | bytes 24580

commit v2 on v1

v2 whole, which is shorter than its diff:
```python
import functools
import math

import jax
import jax.numpy as jnp
from jax import lax
from jax.experimental import pallas as pl
from jax.experimental.pallas import tpu as pltpu
from jax.sharding import PartitionSpec as P

D = 512
H = 16
E = 32
WIN = 144
SLAB = 2 * WIN
TOK = 2 * SLAB
GROUP = 8
LANES = GROUP * WIN
SCALE = 1.0 / math.sqrt(E)
BF = jnp.bfloat16
F32 = jnp.float32
MESH = pl.DeviceIdType.MESH
NN = (((1,), (0,)), ((), ()))
NT = (((1,), (1,)), ((), ()))
TN = (((0,), (0,)), ((), ()))


def mm(a, b, dims=NN):
    return lax.dot_general(a, b, dims, preferred_element_type=F32)


def near(lon, lat):
    n_lon, n_lat = lax.axis_size("lon"), lax.axis_size("lat")
    return ((lax.axis_index("lon") + lon + n_lon) % n_lon, (lax.axis_index("lat") + lat + n_lat) % n_lat)


HALO = ((0, 1), (0, -1), (1, 0), (-1, 0), (1, -1), (-1, 1))
SIZES = {"x": 4, "y": 8, "z": 8}
CUBE = tuple((a, b, c) for a in (1, 0) for b in (1, 0) for c in (1, 0) if a + b + c)
FAR = tuple((a, b, c) for a in (1, 0) for b in (2, 1, 3, 0) for c in (2, 1, 3, 0) if a + b + c)
RELAY = (("y", (2, -2)), ("z", (2, -2)), ("z", (2, -2)), ("x", (2,)))
PARTS = (((0, 2), (2, 4)), ((4, 7), (7, 10)), ((10, 13), (13, 16)))
QKV_BLOCKS = (4, 5, 10, 11, 6, 7, 12, 13, 8, 9, 14, 15)


def position():
    lon, lat = lax.axis_index("lon"), lax.axis_index("lat")
    return {"x": lon // 16, "y": lon % 8, "z": (lat // 2) * 2 + (lon // 8) % 2, "core": lat % 2}


def device(at):
    return (at["x"] * 16 + (at["z"] % 2) * 8 + at["y"], (at["z"] // 2) * 2 + at["core"])


def moved(at, **steps):
    new = dict(at)
    for axis, step in steps.items():
        size = SIZES.get(axis, 2)
        new[axis] = (at[axis] + step + size) % size
    return device(new)


def lane_head():
    return lax.broadcasted_iota(jnp.int32, (WIN, 256), 1) // E


def stack_heads(x):
    lane = lane_head()
    zero = jnp.zeros_like(x)
    return jnp.concatenate([jnp.where(lane == h, x, zero) for h in range(GROUP)], axis=0)


def pick_heads(r):
    lane = lane_head()
    out = r[0:WIN]
    for h in range(1, GROUP):
        out = jnp.where(lane == h, r[h * WIN : (h + 1) * WIN], out)
    return out


def level_order(rows, natural):
    return natural == 4 * (rows % 72) + (rows // 72 + 1) % 4


def owner_order(i, p):
    x = 2 * ((p // 16) % 2) + (p // 128) % 2
    y = 2 * ((p // 4) % 4) + (p // 64) % 2
    return i == x * 128 + ((p // 32) % 2) * 64 + y * 8 + (p % 4) * 2 + p // 256


def one_hot(relation, shape, swap=False):
    a = lax.broadcasted_iota(jnp.int32, shape, 1 if swap else 0)
    b = lax.broadcasted_iota(jnp.int32, shape, 0 if swap else 1)
    return jnp.where(relation(a, b), 1.0, 0.0).astype(BF)


def region(pos, split_level, split_lat):
    return (pos // 72) * split_level + 2 * split_lat * ((pos % 6) // 3)


def signal(sem, to):
    pl.semaphore_signal(sem, inc=1, device_id=to, device_id_type=MESH)


def remote(src, dst, send, recv, to):
    copy = pltpu.make_async_remote_copy(
        src_ref=src, dst_ref=dst, send_sem=send, recv_sem=recv, device_id=to, device_id_type=MESH
    )
    copy.start()
    return copy


def local(src, dst, sem):
    copy = pltpu.make_async_copy(src, dst, sem)
    copy.start()
    return copy


def block_kernel(norm, tok, cot, wqkv, wout, own_path, grad_qkv, grad_out, *scratch):
    (ET, EC, X, XO, C, PR, A, DM, DA, DP, PT, path, G, R0, RC, F, Q) = scratch[:17]
    (hs, hr, hl, bs, br, bl, s0, r0, sc, rc, sf, rf, relay) = scratch[17:]
    at = position()
    bit = {axis: at[axis] % 2 for axis in SIZES}
    core = at["core"]
    lat = lax.axis_index("lat")
    last = lax.axis_size("lat") - 1

    greeted = [near(*step) for step in HALO] + [moved(at, core=1)]
    for a, b, c in CUBE:
        for sense in (1, -1):
            steps = {axis: sense * far * (1 - 2 * bit[axis]) for axis, far in (("x", a), ("y", b), ("z", c))}
            greeted.append(moved(at, **steps))
    greeted += [moved(at, **{axis: step}) for axis, steps in RELAY[1:] + RELAY[:1] for step in steps][2:]
    barrier = pltpu.get_barrier_semaphore()
    for other in greeted:
        signal(barrier, other)
    pl.semaphore_wait(barrier, len(greeted))

    come = []
    for a, (src, ext) in enumerate(((tok, ET), (cot, EC))):
        come.append(
            (
                local(src.at[6:18, 3:6], ext.at[0, :, 0:3], hl.at[a, 0]),
                remote(src.at[6:18, 0:3], ext.at[0, :, 3:6], hs.at[a, 0], hr.at[a, 0], near(0, -1)),
            )
        )
        come.append(
            (
                local(src.at[18:24, 0:3], ext.at[1, 0:6, 3:6], hl.at[a, 1]),
                remote(src.at[18:24, 3:6], ext.at[1, 0:6, 0:3], hs.at[a, 1], hr.at[a, 1], near(0, 1)),
                remote(src.at[0:6, 3:6], ext.at[1, 6:12, 0:3], hs.at[a, 2], hr.at[a, 2], near(-1, 1)),
                remote(src.at[0:6, 0:3], ext.at[1, 6:12, 3:6], hs.at[a, 3], hr.at[a, 3], near(-1, 0)),
            )
        )

    def relay_send(n):
        axis, steps = RELAY[n]
        for step in steps:
            signal(relay.at[n], moved(at, **{axis: step}))

    def relay_wait(n):
        pl.semaphore_wait(relay.at[n], len(RELAY[n][1]))

    relay_send(0)
    order = one_hot(level_order, (SLAB, SLAB))
    owner = one_hot(owner_order, (D, D), swap=True)

    def parts(rows, g):
        return [PR[rows, c * D + g * 256 : c * D + (g + 1) * 256] for c in range(3)]

    def forward(i, _):
        rows = pl.ds(pl.multiple_of(i * WIN, WIN), WIN)
        split_lat = jnp.where(lat == jnp.where(i < 2, last, 0), 1, 0)
        key_region = region(lax.broadcasted_iota(jnp.int32, (WIN, 128), 0), i % 2, split_lat)
        for g in range(2):
            q, k, v = parts(rows, g)
            scores = mm(k, stack_heads(q), NT)
            probs_b = []
            for c in range(LANES // 128):
                cols = slice(c * 128, (c + 1) * 128)
                pos = lax.broadcasted_iota(jnp.int32, (1, 128), 1) + c * 128
                allowed = key_region == region(pos % WIN, i % 2, split_lat)
                s = jnp.where(allowed, scores[:, cols] * SCALE, -1e30)
                e = jnp.exp(s - jnp.max(s, axis=0, keepdims=True))
                p = e * (1.0 / jnp.sum(e, axis=0, keepdims=True))
                PT[i * 2 + g, :, cols] = p
                probs_b.append(p.astype(BF))
            probs_b = jnp.concatenate(probs_b, axis=1)
            A[rows, g * 256 : (g + 1) * 256] = pick_heads(mm(probs_b, v, TN)).astype(BF)
        return 0

    for w in range(2):
        for copy in come[w]:
            copy.wait()
        rows = pl.ds(w * SLAB, SLAB)
        X[rows, :] = mm(order, ET[w].reshape(SLAB, D)).astype(BF)
        for c in range(3):
            cols = pl.ds(c * D, D)
            PR[rows, cols] = mm(X[rows, :], wqkv[:, cols]).astype(BF)
        lax.fori_loop(2 * w, 2 * w + 2, forward, 0)
        relay_wait(w)
        relay_send(w + 1)

    XO[...] = mm(owner, X[...], NT).astype(BF)
    for w in range(2):
        for copy in come[2 + w]:
            copy.wait()
        rows = pl.ds(w * SLAB, SLAB)
        C[rows, :] = mm(order, EC[w].reshape(SLAB, D)).astype(BF)
    for i in range(4):
        rows = pl.ds(i * WIN, WIN)
        mixed = mm(A[rows, :], wout[...])
        centred = mixed - jnp.mean(mixed, axis=-1, keepdims=True)
        rstd = lax.rsqrt(jnp.mean(centred * centred, axis=-1, keepdims=True) + 1e-5)
        normed = centred * rstd
        up = C[rows, :].astype(F32)
        d_mixed = rstd * (
            up - jnp.mean(up, axis=-1, keepdims=True) - normed * jnp.mean(up * normed, axis=-1, keepdims=True)
        )
        d_mixed = d_mixed.astype(BF)
        DM[rows, :] = d_mixed
        DA[rows, :] = mm(d_mixed, wout[...], NT).astype(BF)

    sent = []

    def span(lo, hi):
        return pl.ds(lo * 128, (hi - lo) * 128)

    def to_core(part):
        return [
            remote(
                G.at[1 - core, :, :, :, :, span(lo, hi)],
                R0.at[:, :, :, :, span(lo, hi)],
                s0.at[part, n],
                r0.at[part, n],
                moved(at, core=1),
            )
            for n, (lo, hi) in enumerate(PARTS[part])
        ]

    def to_cube(part, flying):
        out = []
        for n, (lo, hi) in enumerate(PARTS[part]):
            flying[n].wait_recv()
            sent.append(flying[n])
            cols = span(lo, hi)
            G[core, :, :, :, :, cols] = G[core, :, :, :, :, cols] + R0[:, :, :, :, cols]
            for k, (a, b, c) in enumerate(CUBE):
                steps = {
                    axis: far * (1 - 2 * n) * (1 - 2 * bit[axis]) for axis, far in (("x", a), ("y", b), ("z", c)) if far
                }
                place = [1 - bit[axis] if far else bit[axis] for axis, far in (("x", a), ("y", b), ("z", c))]
                out.append(
                    remote(
                        G.at[core, place[0], place[1], place[2], :, cols],
                        RC.at[k, :, cols],
                        sc.at[part, n, k],
                        rc.at[part, n, k],
                        moved(at, **steps),
                    )
                )
        return out

    def take_cube(part, flying):
        for copy in flying:
            copy.wait_recv()
        sent.extend(flying)
        for c in range(PARTS[part][0][0], PARTS[part][1][1]):
            cols = span(c, c + 1)
            value = G[core, bit["x"], bit["y"], bit["z"], :, cols]
            for k in range(len(CUBE)):
                value = value + RC[k, :, cols]
            F[c // 8, pl.ds(c % 8, 32, stride=8), :] = value

    def row(a, b, c):
        place = ((at["x"] // 2 + a) % 2) * 16 + ((at["y"] // 2 + b) % 4) * 4 + (at["z"] // 2 + c) % 4
        return pl.ds(pl.multiple_of(place * 8, 8), 8)

    def to_far(half):
        return [
            remote(
                F.at[half, row(a, b, c)],
                Q.at[half, n],
                sf.at[half, n],
                rf.at[half, n],
                moved(at, x=2 * a, y=2 * b, z=2 * c),
            )
            for n, (a, b, c) in enumerate(FAR)
        ]

    def take_far(half, flying):
        value = F[half, row(0, 0, 0), :]
        for n, copy in enumerate(flying):
            copy.wait_recv()
            value = value + Q[half, n]
        sent.extend(flying)
        return value * norm

    def backward(g, i, _):
        rows = pl.ds(pl.multiple_of(i * WIN, WIN), WIN)
        q, k, v = parts(rows, g)
        d_att = stack_heads(DA[rows, g * 256 : (g + 1) * 256])
        d_probs = mm(v, d_att, NT)
        probs_b, d_scores = [], []
        for c in range(LANES // 128):
            cols = slice(c * 128, (c + 1) * 128)
            p = PT[i * 2 + g, :, cols]
            dp = d_probs[:, cols]
            probs_b.append(p.astype(BF))
            d_scores.append((p * (dp - jnp.sum(dp * p, axis=0, keepdims=True)) * SCALE).astype(BF))
        probs_b = jnp.concatenate(probs_b, axis=1)
        d_scores = jnp.concatenate(d_scores, axis=1)
        d_parts = (pick_heads(mm(d_scores, k, TN)), mm(d_scores, stack_heads(q)), mm(probs_b, d_att))
        for c, part in enumerate(d_parts):
            DP[rows, c * D + g * 256 : c * D + (g + 1) * 256] = part.astype(BF)
        return 0

    def weight_grad(g):
        for c in range(3):
            G[:, :, :, :, :, span(4 + 6 * g + 2 * c, 6 + 6 * g + 2 * c)] = mm(
                XO[...], DP[:, c * D + g * 256 : c * D + (g + 1) * 256]
            ).reshape(2, 2, 2, 2, 32, 256)

    G[:, :, :, :, :, 0:D] = mm(mm(owner, A[...], NT).astype(BF), DM[...]).reshape(2, 2, 2, 2, 32, D)
    core_out = to_core(0)
    relay_wait(2)
    relay_send(3)
    lax.fori_loop(0, 2, functools.partial(backward, 0), 0)
    cube_out = to_cube(0, core_out)
    lax.fori_loop(2, 4, functools.partial(backward, 0), 0)
    weight_grad(0)
    core_first = to_core(1)
    relay_wait(3)
    lax.fori_loop(0, 2, functools.partial(backward, 1), 0)
    cube_first = to_cube(1, core_first)
    take_cube(0, cube_out)
    lax.fori_loop(2, 4, functools.partial(backward, 1), 0)
    weight_grad(1)
    core_second = to_core(2)

    back = one_hot(level_order, (SLAB, SLAB), swap=True)
    backs = []
    for w in range(2):
        grads = mm(DP[pl.ds(w * SLAB, SLAB), :], wqkv[...], NT).astype(BF)
        path[w] = mm(back, grads).astype(BF).reshape(path.shape[1:])
        if w == 0:
            backs += [
                remote(path.at[0, :, 3:6], own_path.at[6:18, 0:3], bs.at[0], br.at[0], near(0, 1)),
                local(path.at[0, :, 0:3], own_path.at[6:18, 3:6], bl.at[0]),
            ]
        else:
            backs += [
                remote(path.at[1, 0:6, 0:3], own_path.at[18:24, 3:6], bs.at[1], br.at[1], near(0, -1)),
                remote(path.at[1, 6:12, 0:3], own_path.at[0:6, 3:6], bs.at[2], br.at[2], near(1, -1)),
                remote(path.at[1, 6:12, 3:6], own_path.at[0:6, 0:3], bs.at[3], br.at[3], near(1, 0)),
                local(path.at[1, 0:6, 3:6], own_path.at[18:24, 0:3], bl.at[1]),
            ]

    cube_second = to_cube(2, core_second)
    take_cube(1, cube_first)
    far_first = to_far(0)
    take_cube(2, cube_second)
    far_second = to_far(1)
    low = take_far(0, far_first)
    high = take_far(1, far_second)
    grad_out[...] = low[0:4]
    for n, block in enumerate(QKV_BLOCKS):
        grad_qkv[n : n + 1, :] = (low, high)[block // 8][block % 8 : block % 8 + 1]
    for copy in sent:
        copy.wait_send()
    for copy in backs:
        copy.wait()


def block(tok, cot, wqkv, wout, norm):
    vm = pl.BlockSpec(memory_space=pltpu.VMEM)
    any_ = pl.BlockSpec(memory_space=pl.ANY)
    rows = pltpu.VMEM((TOK, D), BF)
    wide = pltpu.VMEM((TOK, 3 * D), BF)
    ext = pltpu.VMEM((2, 12, 6, 4, D), BF)
    dma = pltpu.SemaphoreType.DMA
    return pl.pallas_call(
        functools.partial(block_kernel, norm),
        out_shape=(
            jax.ShapeDtypeStruct(tok.shape, BF),
            jax.ShapeDtypeStruct((12, 128), F32),
            jax.ShapeDtypeStruct((4, 128), F32),
        ),
        in_specs=[any_, any_, vm, vm],
        out_specs=(vm,) * 3,
        scratch_shapes=[
            ext,
            ext,
            rows,
            pltpu.VMEM((D, TOK), BF),
            rows,
            wide,
            rows,
            rows,
            rows,
            wide,
            pltpu.VMEM((8, WIN, LANES), F32),
            ext,
            pltpu.VMEM((2, 2, 2, 2, 32, 4 * D), F32),
            pltpu.VMEM((2, 2, 2, 32, 4 * D), F32),
            pltpu.VMEM((len(CUBE), 32, 4 * D), F32),
            pltpu.VMEM((2, 32 * 8, 128), F32),
            pltpu.VMEM((2, len(FAR), 8, 128), F32),
            dma((2, 4)),
            dma((2, 4)),
            dma((2, 2)),
            dma((4,)),
            dma((4,)),
            dma((2,)),
            dma((3, 2)),
            dma((3, 2)),
            dma((3, 2, len(CUBE))),
            dma((3, 2, len(CUBE))),
            dma((2, len(FAR))),
            dma((2, len(FAR))),
            pltpu.SemaphoreType.REGULAR((len(RELAY),)),
        ],
        compiler_params=pltpu.CompilerParams(collective_id=0, has_side_effects=True, vmem_limit_bytes=56 * 2**20),
        name="block",
    )(tok, cot, wqkv, wout)


def body(tokens, cotangent, w_qkv, w_out):
    count = tokens.shape[0] * tokens.shape[1] * tokens.shape[2] * lax.axis_size("lon") * lax.axis_size("lat")
    own_path, grad_qkv, grad_out = block(tokens, cotangent, w_qkv, w_out, 1.0 / math.sqrt(count))
    grad_tokens = (cotangent.astype(F32) + own_path.astype(F32)).astype(BF)
    return grad_tokens, grad_qkv.reshape(-1), grad_out.reshape(-1)


def solution(mesh):
    in_specs = (P("lon", "lat", None, None), P("lon", "lat", None, None), P(), P())
    out_specs = (P("lon", "lat", None, None), P(("lon", "lat")), P(("lon", "lat")))
    return jax.shard_map(body, mesh=mesh, in_specs=in_specs, out_specs=out_specs, check_vma=False)
```

time: 94.2 us -> 77.5 us (0.82)
  Pallas kernels: 89.4 us -> 73.3 us
    pallas_call x3 -> x1, Pallas kernels: 89.4 us -> 73.3 us  [block(): pl.pallas_call(functools.partial(block_kernel, norm), out_shape=(jax.Shap...]
    unnamed x4 -> x8, local copies, waits for them, and re-layouts: 0.01 us -> 1.19 us
    slice x2 -> x0, local copies, waits for them, and re-layouts: 1.18 us -> none  [body(): return (grad_tokens, total[:3 * D], total[3 * D:])]
where the time goes in v2:
time: 77.5 us; the launch traced here: 77.3 us
  Pallas kernels  73.3 us (95%)
  other arithmetic  2.19 us (3%)
  local copies, waits for them, and re-layouts  1.19 us (2%)
    pallas_call x1, Pallas kernels, block(): pl.pallas_call(functools.partial(block_kernel, norm), out_shape=(jax.Shap...  73.3 us
    convert_element_type x1, other arithmetic, body(): grad_tokens = (cotangent.astype(F32) + own_path.astype(F32)).astype(BF)  2.19 us

profile of v2, /device:TPU:1, one launch (start us, length us, event | category | flops | bytes accessed | tf_op | source)
XLA Modules:
  0.0 77.3 jit_solution(10894751558602493714)
XLA Ops:
  0.6 0.0 copy-start
  0.6 73.3 %block.1 = (bf16[24,6,4,512]{3,2,1,0:T(4,128)(2,1)}, f32[12,128]{1,0:T(8,128)}, f32[4,128]{1,0:T(4,128)}) custom-call(bf16[24,6,4,512]{3,2,1,0:T(4,128)(2,1)} %tok.1, bf16[24,6,4,512]{3,2,1,0:T(4,128)(2,1)} %cot.1, bf16[512,1536]{1,0:T(8,128)(2,1)} %wqkv.1, bf16[512,512]{1,0:T(8,128)(2,1)} %wout.1), custom_call_target="tpu_custom_call" | custom-call | tf_op jit(solution)/shard_map/block/pallas_call | solution.py:382
  73.9 0.0 copy-start.1
  73.9 0.0 copy-start.2
  73.9 0.0 copy-done
  73.9 2.2 %add_convert_fusion = bf16[24,6,4,512]{3,2,1,0:T(4,128)(2,1)} fusion(bf16[24,6,4,512]{3,2,1,0:T(4,128)(2,1)} %get-tuple-element.6, bf16[24,6,4,512]{3,2,1,0:T(4,128)(2,1)S(1)} %copy-done), kind=kLoop, calls=%fused_computation | loop fusion | flops 1179648 | bytes 1769472 | tf_op jit(solution)/shard_map/convert_element_type | solution.py:431
  76.1 0.0 copy-done.1
  76.1 0.6 copy.9
  76.7 0.0 copy-done.2
  76.7 0.6 copy.10
Async XLA Ops:
  0.6 73.3 %copy-start = (bf16[24,6,4,512]{3,2,1,0:T(4,128)(2,1)S(1)}, bf16[24,6,4,512]{3,2,1,0:T(4,128)(2,1)}, u32[]{:S(2)}) copy-start(bf16[24,6,4,512]{3,2,1,0:T(4,128)(2,1)} %cot.1) | copy-start | bytes 1769476
  73.9 2.2 %copy-start.1 = (f32[12,128]{1,0:T(8,128)S(1)}, f32[12,128]{1,0:T(8,128)}, u32[]{:S(2)}) copy-start(f32[12,128]{1,0:T(8,128)} %get-tuple-element.7) | copy-start | bytes 18436
  73.9 2.8 %copy-start.2 = (f32[4,128]{1,0:T(4,128)S(1)}, f32[4,128]{1,0:T(4,128)}, u32[]{:S(2)}) copy-start(f32[4,128]{1,0:T(4,128)} %get-tuple-element.8) | copy-start | bytes 6148

commit v3 on v2

--- a/solution.py
+++ b/solution.py
@@ -116,9 +116,9 @@
     return copy
 
 
-def block_kernel(norm, tok, cot, wqkv, wout, own_path, grad_qkv, grad_out, *scratch):
-    (ET, EC, X, XO, C, PR, A, DM, DA, DP, PT, path, G, R0, RC, F, Q) = scratch[:17]
-    (hs, hr, hl, bs, br, bl, s0, r0, sc, rc, sf, rf, relay) = scratch[17:]
+def block_kernel(norm, tok, cot, wqkv_in, wout_in, grad_tok, grad_qkv, grad_out, *scratch):
+    (wqkv, wout, CT, own_path, ET, EC, X, XO, C, PR, A, DM, DA, DP, PT, path, G, R0, CB, RC, F, Q) = scratch[:22]
+    (ws, hs, hr, hl, bs, br, bl, s0, r0, sc, rc, sf, rf, relay) = scratch[22:]
     at = position()
     bit = {axis: at[axis] % 2 for axis in SIZES}
     core = at["core"]
@@ -134,6 +134,7 @@
     barrier = pltpu.get_barrier_semaphore()
     for other in greeted:
         signal(barrier, other)
+    own = [local(wqkv_in, wqkv, ws.at[0]), local(wout_in, wout, ws.at[1]), local(cot, CT, ws.at[2])]
     pl.semaphore_wait(barrier, len(greeted))
 
     come = []
@@ -162,6 +163,7 @@
         pl.semaphore_wait(relay.at[n], len(RELAY[n][1]))
 
     relay_send(0)
+    own[0].wait()
     order = one_hot(level_order, (SLAB, SLAB))
     owner = one_hot(owner_order, (D, D), swap=True)
 
@@ -202,6 +204,7 @@
         relay_send(w + 1)
 
     XO[...] = mm(owner, X[...], NT).astype(BF)
+    own[1].wait()
     for w in range(2):
         for copy in come[2 + w]:
             copy.wait()
@@ -244,7 +247,7 @@
             flying[n].wait_recv()
             sent.append(flying[n])
             cols = span(lo, hi)
-            G[core, :, :, :, :, cols] = G[core, :, :, :, :, cols] + R0[:, :, :, :, cols]
+            CB[:, :, :, :, cols] = (G[core, :, :, :, :, cols] + R0[:, :, :, :, cols]).astype(BF)
             for k, (a, b, c) in enumerate(CUBE):
                 steps = {
                     axis: far * (1 - 2 * n) * (1 - 2 * bit[axis]) for axis, far in (("x", a), ("y", b), ("z", c)) if far
@@ -252,7 +255,7 @@
                 place = [1 - bit[axis] if far else bit[axis] for axis, far in (("x", a), ("y", b), ("z", c))]
                 out.append(
                     remote(
-                        G.at[core, place[0], place[1], place[2], :, cols],
+                        CB.at[place[0], place[1], place[2], :, cols],
                         RC.at[k, :, cols],
                         sc.at[part, n, k],
                         rc.at[part, n, k],
@@ -267,9 +270,9 @@
         sent.extend(flying)
         for c in range(PARTS[part][0][0], PARTS[part][1][1]):
             cols = span(c, c + 1)
-            value = G[core, bit["x"], bit["y"], bit["z"], :, cols]
+            value = G[core, bit["x"], bit["y"], bit["z"], :, cols] + R0[bit["x"], bit["y"], bit["z"], :, cols]
             for k in range(len(CUBE)):
-                value = value + RC[k, :, cols]
+                value = value + RC[k, :, cols].astype(F32)
             F[c // 8, pl.ds(c % 8, 32, stride=8), :] = value
 
     def row(a, b, c):
@@ -361,6 +364,16 @@
     far_first = to_far(0)
     take_cube(2, cube_second)
     far_second = to_far(1)
+    for copy in backs:
+        copy.wait()
+    own[2].wait()
+
+    def add(i, _):
+        CT[i] = (CT[i].astype(F32) + own_path[i].astype(F32)).astype(BF)
+        return 0
+
+    lax.fori_loop(0, CT.shape[0], add, 0)
+    out = local(CT, grad_tok, ws.at[3])
     low = take_far(0, far_first)
     high = take_far(1, far_second)
     grad_out[...] = low[0:4]
@@ -368,8 +381,7 @@
         grad_qkv[n : n + 1, :] = (low, high)[block // 8][block % 8 : block % 8 + 1]
     for copy in sent:
         copy.wait_send()
-    for copy in backs:
-        copy.wait()
+    out.wait()
 
 
 def block(tok, cot, wqkv, wout, norm):
@@ -386,9 +398,13 @@
             jax.ShapeDtypeStruct((12, 128), F32),
             jax.ShapeDtypeStruct((4, 128), F32),
         ),
-        in_specs=[any_, any_, vm, vm],
-        out_specs=(vm,) * 3,
+        in_specs=[any_] * 4,
+        out_specs=(any_, vm, vm),
         scratch_shapes=[
+            pltpu.VMEM(wqkv.shape, BF),
+            pltpu.VMEM(wout.shape, BF),
+            pltpu.VMEM(tok.shape, BF),
+            pltpu.VMEM(tok.shape, BF),
             ext,
             ext,
             rows,
@@ -403,9 +419,11 @@
             ext,
             pltpu.VMEM((2, 2, 2, 2, 32, 4 * D), F32),
             pltpu.VMEM((2, 2, 2, 32, 4 * D), F32),
-            pltpu.VMEM((len(CUBE), 32, 4 * D), F32),
+            pltpu.VMEM((2, 2, 2, 32, 4 * D), BF),
+            pltpu.VMEM((len(CUBE), 32, 4 * D), BF),
             pltpu.VMEM((2, 32 * 8, 128), F32),
             pltpu.VMEM((2, len(FAR), 8, 128), F32),
+            dma((4,)),
             dma((2, 4)),
             dma((2, 4)),
             dma((2, 2)),
@@ -427,8 +445,7 @@
 
 def body(tokens, cotangent, w_qkv, w_out):
     count = tokens.shape[0] * tokens.shape[1] * tokens.shape[2] * lax.axis_size("lon") * lax.axis_size("lat")
-    own_path, grad_qkv, grad_out = block(tokens, cotangent, w_qkv, w_out, 1.0 / math.sqrt(count))
-    grad_tokens = (cotangent.astype(F32) + own_path.astype(F32)).astype(BF)
+    grad_tokens, grad_qkv, grad_out = block(tokens, cotangent, w_qkv, w_out, 1.0 / math.sqrt(count))
     return grad_tokens, grad_qkv.reshape(-1), grad_out.reshape(-1)
 
 

time: 77.5 us -> 75 us (0.968); the launches traced: 77.3 us -> 73.6 us
  Pallas kernels: 73.3 us -> 68.3 us
  local copies, waits for them, and re-layouts: 1.19 us -> 4.62 us
  other arithmetic: 2.19 us -> 0 us
    pallas_call x1, Pallas kernels: 73.3 us -> 68.3 us  [block(): pl.pallas_call(functools.partial(block_kernel, norm), out_shape=(jax.Shap...]
    unnamed x8 -> x3, local copies, waits for them, and re-layouts: 1.19 us -> 4.62 us
    convert_element_type x1 -> x0, other arithmetic: 2.19 us -> none  [body(): grad_tokens = (cotangent.astype(F32) + own_path.astype(F32)).astype(BF)]
where the time goes in v3:
time: 75 us; the launch traced here: 73.6 us
  Pallas kernels  68.3 us (91%)
  local copies, waits for them, and re-layouts  4.62 us (6%)
    pallas_call x1, Pallas kernels, block(): pl.pallas_call(functools.partial(block_kernel, norm), out_shape=(jax.Shap...  68.3 us
    unnamed x3, local copies, waits for them, and re-layouts  4.62 us

profile of v3, /device:TPU:1, one launch (start us, length us, event | category | flops | bytes accessed | tf_op | source)
XLA Modules:
  0.0 73.6 jit_solution(8080176739820946832)
XLA Ops:
  0.6 68.3 %block.1 = (bf16[24,6,4,512]{3,2,1,0:T(4,128)(2,1)}, f32[12,128]{1,0:T(8,128)}, f32[4,128]{1,0:T(4,128)}) custom-call(bf16[24,6,4,512]{3,2,1,0:T(4,128)(2,1)} %tok.1, bf16[24,6,4,512]{3,2,1,0:T(4,128)(2,1)} %cot.1, bf16[512,1536]{1,0:T(8,128)(2,1)} %wqkv_in.1, bf16[512,512]{1,0:T(8,128)(2,1)} %wout_in.1), custom_call_target="tpu_custom_call" | custom-call | tf_op jit(solution)/shard_map/block/pallas_call | solution.py:394
  68.9 2.1 %copy.10 = bf16[24,6,4,512]{3,2,1,0:T(4,128)(2,1)} copy(bf16[24,6,4,512]{3,2,1,0:T(4,128)(2,1)} %get-tuple-element.12) | data formatting | bytes 1179648
  71.0 1.3 %copy.11 = f32[1536]{0:T(1024)} copy(f32[1536]{0:T(1024)} %bitcast.2) | data formatting | bytes 12288
  72.3 1.2 %copy.12 = f32[512]{0:T(512)} copy(f32[512]{0:T(512)} %bitcast.3) | data formatting | bytes 4096

commit v4 on v3

--- a/solution.py
+++ b/solution.py
@@ -39,8 +39,8 @@
 CUBE = tuple((a, b, c) for a in (1, 0) for b in (1, 0) for c in (1, 0) if a + b + c)
 FAR = tuple((a, b, c) for a in (1, 0) for b in (2, 1, 3, 0) for c in (2, 1, 3, 0) if a + b + c)
 RELAY = (("y", (2, -2)), ("z", (2, -2)), ("z", (2, -2)), ("x", (2,)))
-PARTS = (((0, 2), (2, 4)), ((4, 7), (7, 10)), ((10, 13), (13, 16)))
-QKV_BLOCKS = (4, 5, 10, 11, 6, 7, 12, 13, 8, 9, 14, 15)
+PARTS = (((0, 2), (2, 4)), ((4, 8), (8, 12)), ((12, 14), (14, 16)))
+QKV_BLOCKS = (4, 5, 12, 13, 6, 7, 14, 15, 8, 9, 10, 11)
 
 
 def position():
@@ -170,9 +170,9 @@
     def parts(rows, g):
         return [PR[rows, c * D + g * 256 : c * D + (g + 1) * 256] for c in range(3)]
 
-    def forward(i, _):
-        rows = pl.ds(pl.multiple_of(i * WIN, WIN), WIN)
-        split_lat = jnp.where(lat == jnp.where(i < 2, last, 0), 1, 0)
+    def forward(i):
+        rows = pl.ds(i * WIN, WIN)
+        split_lat = jnp.where(lat == (last if i < 2 else 0), 1, 0)
         key_region = region(lax.broadcasted_iota(jnp.int32, (WIN, 128), 0), i % 2, split_lat)
         for g in range(2):
             q, k, v = parts(rows, g)
@@ -189,7 +189,6 @@
                 probs_b.append(p.astype(BF))
             probs_b = jnp.concatenate(probs_b, axis=1)
             A[rows, g * 256 : (g + 1) * 256] = pick_heads(mm(probs_b, v, TN)).astype(BF)
-        return 0
 
     for w in range(2):
         for copy in come[w]:
@@ -199,7 +198,8 @@
         for c in range(3):
             cols = pl.ds(c * D, D)
             PR[rows, cols] = mm(X[rows, :], wqkv[:, cols]).astype(BF)
-        lax.fori_loop(2 * w, 2 * w + 2, forward, 0)
+        for i in range(2 * w, 2 * w + 2):
+            forward(i)
         relay_wait(w)
         relay_send(w + 1)
 
@@ -299,8 +299,8 @@
         sent.extend(flying)
         return value * norm
 
-    def backward(g, i, _):
-        rows = pl.ds(pl.multiple_of(i * WIN, WIN), WIN)
+    def backward(g, i):
+        rows = pl.ds(i * WIN, WIN)
         q, k, v = parts(rows, g)
         d_att = stack_heads(DA[rows, g * 256 : (g + 1) * 256])
         d_probs = mm(v, d_att, NT)
@@ -311,55 +311,52 @@
             dp = d_probs[:, cols]
             probs_b.append(p.astype(BF))
             d_scores.append((p * (dp - jnp.sum(dp * p, axis=0, keepdims=True)) * SCALE).astype(BF))
-        probs_b = jnp.concatenate(probs_b, axis=1)
         d_scores = jnp.concatenate(d_scores, axis=1)
-        d_parts = (pick_heads(mm(d_scores, k, TN)), mm(d_scores, stack_heads(q)), mm(probs_b, d_att))
-        for c, part in enumerate(d_parts):
+        for c, part in enumerate((pick_heads(mm(d_scores, k, TN)), mm(d_scores, stack_heads(q)))):
             DP[rows, c * D + g * 256 : c * D + (g + 1) * 256] = part.astype(BF)
-        return 0
-
-    def weight_grad(g):
-        for c in range(3):
-            G[:, :, :, :, :, span(4 + 6 * g + 2 * c, 6 + 6 * g + 2 * c)] = mm(
-                XO[...], DP[:, c * D + g * 256 : c * D + (g + 1) * 256]
-            ).reshape(2, 2, 2, 2, 32, 256)
+        if g == 0:
+            d_values = [mm(jnp.concatenate(probs_b, axis=1), d_att)]
+            d_values.append(mm(PT[i * 2 + 1].astype(BF), stack_heads(DA[rows, 256:D])))
+            DP[rows, 2 * D : 3 * D] = jnp.concatenate(d_values, axis=1).astype(BF)
+
+    def weight_grad(block, lo, hi):
+        G[:, :, :, :, :, span(block, block + (hi - lo) // 128)] = mm(XO[...], DP[:, lo:hi]).reshape(
+            2, 2, 2, 2, 32, hi - lo
+        )
 
     G[:, :, :, :, :, 0:D] = mm(mm(owner, A[...], NT).astype(BF), DM[...]).reshape(2, 2, 2, 2, 32, D)
     core_out = to_core(0)
     relay_wait(2)
     relay_send(3)
-    lax.fori_loop(0, 2, functools.partial(backward, 0), 0)
+    for i in range(4):
+        backward(0, i)
     cube_out = to_cube(0, core_out)
-    lax.fori_loop(2, 4, functools.partial(backward, 0), 0)
-    weight_grad(0)
+    weight_grad(4, 0, 256)
+    weight_grad(6, D, D + 256)
+    weight_grad(8, 2 * D, 3 * D)
     core_first = to_core(1)
     relay_wait(3)
-    lax.fori_loop(0, 2, functools.partial(backward, 1), 0)
+    for i in range(4):
+        backward(1, i)
+    weight_grad(12, 256, D)
+    weight_grad(14, D + 256, 2 * D)
+    core_second = to_core(2)
     cube_first = to_cube(1, core_first)
-    take_cube(0, cube_out)
-    lax.fori_loop(2, 4, functools.partial(backward, 1), 0)
-    weight_grad(1)
-    core_second = to_core(2)
 
     back = one_hot(level_order, (SLAB, SLAB), swap=True)
-    backs = []
     for w in range(2):
         grads = mm(DP[pl.ds(w * SLAB, SLAB), :], wqkv[...], NT).astype(BF)
         path[w] = mm(back, grads).astype(BF).reshape(path.shape[1:])
-        if w == 0:
-            backs += [
-                remote(path.at[0, :, 3:6], own_path.at[6:18, 0:3], bs.at[0], br.at[0], near(0, 1)),
-                local(path.at[0, :, 0:3], own_path.at[6:18, 3:6], bl.at[0]),
-            ]
-        else:
-            backs += [
-                remote(path.at[1, 0:6, 0:3], own_path.at[18:24, 3:6], bs.at[1], br.at[1], near(0, -1)),
-                remote(path.at[1, 6:12, 0:3], own_path.at[0:6, 3:6], bs.at[2], br.at[2], near(1, -1)),
-                remote(path.at[1, 6:12, 3:6], own_path.at[0:6, 0:3], bs.at[3], br.at[3], near(1, 0)),
-                local(path.at[1, 0:6, 3:6], own_path.at[18:24, 0:3], bl.at[1]),
-            ]
-
     cube_second = to_cube(2, core_second)
+    take_cube(0, cube_out)
+    backs = [
+        remote(path.at[0, :, 3:6], own_path.at[6:18, 0:3], bs.at[0], br.at[0], near(0, 1)),
+        remote(path.at[1, 0:6, 0:3], own_path.at[18:24, 3:6], bs.at[1], br.at[1], near(0, -1)),
+        remote(path.at[1, 6:12, 0:3], own_path.at[0:6, 3:6], bs.at[2], br.at[2], near(1, -1)),
+        remote(path.at[1, 6:12, 3:6], own_path.at[0:6, 0:3], bs.at[3], br.at[3], near(1, 0)),
+        local(path.at[0, :, 0:3], own_path.at[6:18, 3:6], bl.at[0]),
+        local(path.at[1, 0:6, 3:6], own_path.at[18:24, 0:3], bl.at[1]),
+    ]
     take_cube(1, cube_first)
     far_first = to_far(0)
     take_cube(2, cube_second)

time: 75 us -> 69.7 us (0.929); the launches traced: 73.6 us -> 69.4 us
  Pallas kernels: 68.3 us -> 64.1 us
    pallas_call x1, Pallas kernels: 68.3 us -> 64.1 us  [block(): pl.pallas_call(functools.partial(block_kernel, norm), out_shape=(jax.Shap...]
where the time goes in v4:
time: 69.7 us; the launch traced here: 69.4 us
  Pallas kernels  64.1 us (92%)
  local copies, waits for them, and re-layouts  4.62 us (7%)
    pallas_call x1, Pallas kernels, block(): pl.pallas_call(functools.partial(block_kernel, norm), out_shape=(jax.Shap...  64.1 us
    unnamed x3, local copies, waits for them, and re-layouts  4.62 us

profile of v4, /device:TPU:1, one launch (start us, length us, event | category | flops | bytes accessed | tf_op | source)
XLA Modules:
  0.0 69.4 jit_solution(6121907713851346521)
XLA Ops:
  0.6 64.1 %block.1 = (bf16[24,6,4,512]{3,2,1,0:T(4,128)(2,1)}, f32[12,128]{1,0:T(8,128)}, f32[4,128]{1,0:T(4,128)}) custom-call(bf16[24,6,4,512]{3,2,1,0:T(4,128)(2,1)} %tok.1, bf16[24,6,4,512]{3,2,1,0:T(4,128)(2,1)} %cot.1, bf16[512,1536]{1,0:T(8,128)(2,1)} %wqkv_in.1, bf16[512,512]{1,0:T(8,128)(2,1)} %wout_in.1), custom_call_target="tpu_custom_call" | custom-call | tf_op jit(solution)/shard_map/block/pallas_call | solution.py:391
  64.8 2.1 %copy.10 = bf16[24,6,4,512]{3,2,1,0:T(4,128)(2,1)} copy(bf16[24,6,4,512]{3,2,1,0:T(4,128)(2,1)} %get-tuple-element.12) | data formatting | bytes 1179648
  66.9 1.3 %copy.11 = f32[1536]{0:T(1024)} copy(f32[1536]{0:T(1024)} %bitcast.2) | data formatting | bytes 12288
  68.1 1.2 %copy.12 = f32[512]{0:T(512)} copy(f32[512]{0:T(512)} %bitcast.3) | data formatting | bytes 4096

commit v5 on v4

--- a/solution.py
+++ b/solution.py
@@ -39,8 +39,8 @@
 CUBE = tuple((a, b, c) for a in (1, 0) for b in (1, 0) for c in (1, 0) if a + b + c)
 FAR = tuple((a, b, c) for a in (1, 0) for b in (2, 1, 3, 0) for c in (2, 1, 3, 0) if a + b + c)
 RELAY = (("y", (2, -2)), ("z", (2, -2)), ("z", (2, -2)), ("x", (2,)))
-PARTS = (((0, 2), (2, 4)), ((4, 8), (8, 12)), ((12, 14), (14, 16)))
-QKV_BLOCKS = (4, 5, 12, 13, 6, 7, 14, 15, 8, 9, 10, 11)
+PARTS = (((0, 2), (2, 4)), ((4, 6), (6, 8)), ((8, 10), (10, 12)), ((12, 14), (14, 16)))
+QKV_BLOCKS = (8, 9, 12, 13, 10, 11, 14, 15, 4, 5, 6, 7)
 
 
 def position():
@@ -117,8 +117,8 @@
 
 
 def block_kernel(norm, tok, cot, wqkv_in, wout_in, grad_tok, grad_qkv, grad_out, *scratch):
-    (wqkv, wout, CT, own_path, ET, EC, X, XO, C, PR, A, DM, DA, DP, PT, path, G, R0, CB, RC, F, Q) = scratch[:22]
-    (ws, hs, hr, hl, bs, br, bl, s0, r0, sc, rc, sf, rf, relay) = scratch[22:]
+    (wqkv, wout, CT, own_path, ET, EC, X, XO, C, PR, A, DM, DA, DP, PT, path, G, R0, CB, RC, F, F2, F3, Q, Q2, Q3) = scratch[:26]
+    (ws, hs, hr, hl, bs, br, bl, s0, r0, sc, rc, sf, rf, relay) = scratch[26:]
     at = position()
     bit = {axis: at[axis] % 2 for axis in SIZES}
     core = at["core"]
@@ -225,6 +225,7 @@
         DA[rows, :] = mm(d_mixed, wout[...], NT).astype(BF)
 
     sent = []
+    rows_of = (F, F, F2, F3)
 
     def span(lo, hi):
         return pl.ds(lo * 128, (hi - lo) * 128)
@@ -273,29 +274,28 @@
             value = G[core, bit["x"], bit["y"], bit["z"], :, cols] + R0[bit["x"], bit["y"], bit["z"], :, cols]
             for k in range(len(CUBE)):
                 value = value + RC[k, :, cols].astype(F32)
-            F[c // 8, pl.ds(c % 8, 32, stride=8), :] = value
+            rows_of[c // 4][:, c if c < 8 else c % 4, :] = value
 
     def row(a, b, c):
-        place = ((at["x"] // 2 + a) % 2) * 16 + ((at["y"] // 2 + b) % 4) * 4 + (at["z"] // 2 + c) % 4
-        return pl.ds(pl.multiple_of(place * 8, 8), 8)
-
-    def to_far(half):
+        return ((at["x"] // 2 + a) % 2) * 16 + ((at["y"] // 2 + b) % 4) * 4 + (at["z"] // 2 + c) % 4
+
+    def to_far(n, src, dst):
         return [
             remote(
-                F.at[half, row(a, b, c)],
-                Q.at[half, n],
-                sf.at[half, n],
-                rf.at[half, n],
+                src.at[row(a, b, c)],
+                dst.at[k],
+                sf.at[n, k],
+                rf.at[n, k],
                 moved(at, x=2 * a, y=2 * b, z=2 * c),
             )
-            for n, (a, b, c) in enumerate(FAR)
+            for k, (a, b, c) in enumerate(FAR)
         ]
 
-    def take_far(half, flying):
-        value = F[half, row(0, 0, 0), :]
-        for n, copy in enumerate(flying):
+    def take_far(src, dst, flying):
+        value = src[row(0, 0, 0)]
+        for k, copy in enumerate(flying):
             copy.wait_recv()
-            value = value + Q[half, n]
+            value = value + dst[k]
         sent.extend(flying)
         return value * norm
 
@@ -304,20 +304,22 @@
         q, k, v = parts(rows, g)
         d_att = stack_heads(DA[rows, g * 256 : (g + 1) * 256])
         d_probs = mm(v, d_att, NT)
-        probs_b, d_scores = [], []
+        d_scores = []
         for c in range(LANES // 128):
             cols = slice(c * 128, (c + 1) * 128)
             p = PT[i * 2 + g, :, cols]
             dp = d_probs[:, cols]
-            probs_b.append(p.astype(BF))
             d_scores.append((p * (dp - jnp.sum(dp * p, axis=0, keepdims=True)) * SCALE).astype(BF))
         d_scores = jnp.concatenate(d_scores, axis=1)
         for c, part in enumerate((pick_heads(mm(d_scores, k, TN)), mm(d_scores, stack_heads(q)))):
             DP[rows, c * D + g * 256 : c * D + (g + 1) * 256] = part.astype(BF)
-        if g == 0:
-            d_values = [mm(jnp.concatenate(probs_b, axis=1), d_att)]
-            d_values.append(mm(PT[i * 2 + 1].astype(BF), stack_heads(DA[rows, 256:D])))
-            DP[rows, 2 * D : 3 * D] = jnp.concatenate(d_values, axis=1).astype(BF)
+
+    def values(g, i):
+        rows = pl.ds(i * WIN, WIN)
+        cols = slice(g * 256, (g + 1) * 256)
+        DP[rows, 2 * D + g * 256 : 2 * D + (g + 1) * 256] = mm(
+            PT[i * 2 + g].astype(BF), stack_heads(DA[rows, cols])
+        ).astype(BF)
 
     def weight_grad(block, lo, hi):
         G[:, :, :, :, :, span(block, block + (hi - lo) // 128)] = mm(XO[...], DP[:, lo:hi]).reshape(
@@ -325,30 +327,41 @@
         )
 
     G[:, :, :, :, :, 0:D] = mm(mm(owner, A[...], NT).astype(BF), DM[...]).reshape(2, 2, 2, 2, 32, D)
-    core_out = to_core(0)
+    core_0 = to_core(0)
     relay_wait(2)
     relay_send(3)
     for i in range(4):
+        values(0, i)
+        values(1, i)
+    weight_grad(4, 2 * D, 3 * D)
+    core_1 = to_core(1)
+    for i in range(4):
         backward(0, i)
-    cube_out = to_cube(0, core_out)
-    weight_grad(4, 0, 256)
-    weight_grad(6, D, D + 256)
-    weight_grad(8, 2 * D, 3 * D)
-    core_first = to_core(1)
+    cube_0 = to_cube(0, core_0)
+    weight_grad(8, 0, 256)
+    weight_grad(10, D, D + 256)
+    core_2 = to_core(2)
     relay_wait(3)
     for i in range(4):
         backward(1, i)
+    cube_1 = to_cube(1, core_1)
     weight_grad(12, 256, D)
     weight_grad(14, D + 256, 2 * D)
-    core_second = to_core(2)
-    cube_first = to_cube(1, core_first)
+    core_3 = to_core(3)
+    cube_2 = to_cube(2, core_2)
 
     back = one_hot(level_order, (SLAB, SLAB), swap=True)
     for w in range(2):
         grads = mm(DP[pl.ds(w * SLAB, SLAB), :], wqkv[...], NT).astype(BF)
         path[w] = mm(back, grads).astype(BF).reshape(path.shape[1:])
-    cube_second = to_cube(2, core_second)
-    take_cube(0, cube_out)
+    cube_3 = to_cube(3, core_3)
+    take_cube(0, cube_0)
+    take_cube(1, cube_1)
+    far_1 = to_far(0, F, Q)
+    take_cube(2, cube_2)
+    far_2 = to_far(1, F2, Q2)
+    take_cube(3, cube_3)
+    far_3 = to_far(2, F3, Q3)
     backs = [
         remote(path.at[0, :, 3:6], own_path.at[6:18, 0:3], bs.at[0], br.at[0], near(0, 1)),
         remote(path.at[1, 0:6, 0:3], own_path.at[18:24, 3:6], bs.at[1], br.at[1], near(0, -1)),
@@ -357,10 +370,6 @@
         local(path.at[0, :, 0:3], own_path.at[6:18, 3:6], bl.at[0]),
         local(path.at[1, 0:6, 3:6], own_path.at[18:24, 0:3], bl.at[1]),
     ]
-    take_cube(1, cube_first)
-    far_first = to_far(0)
-    take_cube(2, cube_second)
-    far_second = to_far(1)
     for copy in backs:
         copy.wait()
     own[2].wait()
@@ -371,11 +380,10 @@
 
     lax.fori_loop(0, CT.shape[0], add, 0)
     out = local(CT, grad_tok, ws.at[3])
-    low = take_far(0, far_first)
-    high = take_far(1, far_second)
-    grad_out[...] = low[0:4]
-    for n, block in enumerate(QKV_BLOCKS):
-        grad_qkv[n : n + 1, :] = (low, high)[block // 8][block % 8 : block % 8 + 1]
+    sums = jnp.concatenate([take_far(F, Q, far_1), take_far(F2, Q2, far_2), take_far(F3, Q3, far_3)], axis=0)
+    grad_out[...] = sums[0:4]
+    for n, c in enumerate(QKV_BLOCKS):
+        grad_qkv[n : n + 1, :] = sums[c : c + 1]
     for copy in sent:
         copy.wait_send()
     out.wait()
@@ -418,8 +426,8 @@
             pltpu.VMEM((2, 2, 2, 32, 4 * D), F32),
             pltpu.VMEM((2, 2, 2, 32, 4 * D), BF),
             pltpu.VMEM((len(CUBE), 32, 4 * D), BF),
-            pltpu.VMEM((2, 32 * 8, 128), F32),
-            pltpu.VMEM((2, len(FAR), 8, 128), F32),
+            *(pltpu.VMEM((32, n, 128), F32) for n in (8, 4, 4)),
+            *(pltpu.VMEM((len(FAR), n, 128), F32) for n in (8, 4, 4)),
             dma((4,)),
             dma((2, 4)),
             dma((2, 4)),
@@ -427,12 +435,12 @@
             dma((4,)),
             dma((4,)),
             dma((2,)),
-            dma((3, 2)),
-            dma((3, 2)),
-            dma((3, 2, len(CUBE))),
-            dma((3, 2, len(CUBE))),
-            dma((2, len(FAR))),
-            dma((2, len(FAR))),
+            dma((4, 2)),
+            dma((4, 2)),
+            dma((4, 2, len(CUBE))),
+            dma((4, 2, len(CUBE))),
+            dma((3, len(FAR))),
+            dma((3, len(FAR))),
             pltpu.SemaphoreType.REGULAR((len(RELAY),)),
         ],
         compiler_params=pltpu.CompilerParams(collective_id=0, has_side_effects=True, vmem_limit_bytes=56 * 2**20),

time: 69.7 us -> 71.6 us (1.027)
  Pallas kernels: 64.1 us -> 66 us
    pallas_call x1, Pallas kernels: 64.1 us -> 66 us  [block(): pl.pallas_call(functools.partial(block_kernel, norm), out_shape=(jax.Shap...]
where the time goes in v5:
time: 71.6 us; the launch traced here: 71.3 us
  Pallas kernels  66 us (92%)
  local copies, waits for them, and re-layouts  4.62 us (6%)
    pallas_call x1, Pallas kernels, block(): pl.pallas_call(functools.partial(block_kernel, norm), out_shape=(jax.Shap...  66 us
    unnamed x3, local copies, waits for them, and re-layouts  4.62 us

profile of v5, /device:TPU:1, one launch (start us, length us, event | category | flops | bytes accessed | tf_op | source)
XLA Modules:
  0.0 71.3 jit_solution(1535145904334020106)
XLA Ops:
  0.6 66.0 %block.1 = (bf16[24,6,4,512]{3,2,1,0:T(4,128)(2,1)}, f32[12,128]{1,0:T(8,128)}, f32[4,128]{1,0:T(4,128)}) custom-call(bf16[24,6,4,512]{3,2,1,0:T(4,128)(2,1)} %tok.1, bf16[24,6,4,512]{3,2,1,0:T(4,128)(2,1)} %cot.1, bf16[512,1536]{1,0:T(8,128)(2,1)} %wqkv_in.1, bf16[512,512]{1,0:T(8,128)(2,1)} %wout_in.1), custom_call_target="tpu_custom_call" | custom-call | tf_op jit(solution)/shard_map/block/pallas_call | solution.py:399
  66.7 2.1 %copy.10 = bf16[24,6,4,512]{3,2,1,0:T(4,128)(2,1)} copy(bf16[24,6,4,512]{3,2,1,0:T(4,128)(2,1)} %get-tuple-element.12) | data formatting | bytes 1179648
  68.8 1.3 %copy.11 = f32[1536]{0:T(1024)} copy(f32[1536]{0:T(1024)} %bitcast.2) | data formatting | bytes 12288
  70.0 1.2 %copy.12 = f32[512]{0:T(512)} copy(f32[512]{0:T(512)} %bitcast.3) | data formatting | bytes 4096

commit v6 on v4

--- a/solution.py
+++ b/solution.py
@@ -265,7 +265,7 @@
         return out
 
     def take_cube(part, flying):
-        for copy in flying:
+        for copy in reversed(flying):
             copy.wait_recv()
         sent.extend(flying)
         for c in range(PARTS[part][0][0], PARTS[part][1][1]):
@@ -293,10 +293,9 @@
 
     def take_far(half, flying):
         value = F[half, row(0, 0, 0), :]
-        for n, copy in enumerate(flying):
+        for n, copy in reversed(list(enumerate(flying))):
             copy.wait_recv()
             value = value + Q[half, n]
-        sent.extend(flying)
         return value * norm
 
     def backward(g, i):
@@ -341,12 +340,13 @@
     weight_grad(12, 256, D)
     weight_grad(14, D + 256, 2 * D)
     core_second = to_core(2)
-    cube_first = to_cube(1, core_first)
 
     back = one_hot(level_order, (SLAB, SLAB), swap=True)
     for w in range(2):
         grads = mm(DP[pl.ds(w * SLAB, SLAB), :], wqkv[...], NT).astype(BF)
         path[w] = mm(back, grads).astype(BF).reshape(path.shape[1:])
+        if w == 0:
+            cube_first = to_cube(1, core_first)
     cube_second = to_cube(2, core_second)
     take_cube(0, cube_out)
     backs = [
@@ -372,12 +372,12 @@
     lax.fori_loop(0, CT.shape[0], add, 0)
     out = local(CT, grad_tok, ws.at[3])
     low = take_far(0, far_first)
+    for copy in sent + far_first + far_second:
+        copy.wait_send()
     high = take_far(1, far_second)
     grad_out[...] = low[0:4]
     for n, block in enumerate(QKV_BLOCKS):
         grad_qkv[n : n + 1, :] = (low, high)[block // 8][block % 8 : block % 8 + 1]
-    for copy in sent:
-        copy.wait_send()
     out.wait()
 
 

time: 69.7 us -> 69.6 us (level)
  no operation moved by 1% of the time
where the time goes in v6:
time: 69.6 us; the launch traced here: 69.4 us
  Pallas kernels  64.1 us (92%)
  local copies, waits for them, and re-layouts  4.62 us (7%)
    pallas_call x1, Pallas kernels, block(): pl.pallas_call(functools.partial(block_kernel, norm), out_shape=(jax.Shap...  64.1 us
    unnamed x3, local copies, waits for them, and re-layouts  4.62 us

profile of v6, /device:TPU:1, one launch (start us, length us, event | category | flops | bytes accessed | tf_op | source)
XLA Modules:
  0.0 69.4 jit_solution(13540913671884037248)
XLA Ops:
  0.6 64.1 %block.1 = (bf16[24,6,4,512]{3,2,1,0:T(4,128)(2,1)}, f32[12,128]{1,0:T(8,128)}, f32[4,128]{1,0:T(4,128)}) custom-call(bf16[24,6,4,512]{3,2,1,0:T(4,128)(2,1)} %tok.1, bf16[24,6,4,512]{3,2,1,0:T(4,128)(2,1)} %cot.1, bf16[512,1536]{1,0:T(8,128)(2,1)} %wqkv_in.1, bf16[512,512]{1,0:T(8,128)(2,1)} %wout_in.1), custom_call_target="tpu_custom_call" | custom-call | tf_op jit(solution)/shard_map/block/pallas_call | solution.py:391
  64.8 2.1 %copy.10 = bf16[24,6,4,512]{3,2,1,0:T(4,128)(2,1)} copy(bf16[24,6,4,512]{3,2,1,0:T(4,128)(2,1)} %get-tuple-element.12) | data formatting | bytes 1179648
  66.8 1.3 %copy.11 = f32[1536]{0:T(1024)} copy(f32[1536]{0:T(1024)} %bitcast.2) | data formatting | bytes 12288
  68.1 1.2 %copy.12 = f32[512]{0:T(512)} copy(f32[512]{0:T(512)} %bitcast.3) | data formatting | bytes 4096

commit v7 on v6

--- a/solution.py
+++ b/solution.py
@@ -342,21 +342,25 @@
     core_second = to_core(2)
 
     back = one_hot(level_order, (SLAB, SLAB), swap=True)
+    backs = []
     for w in range(2):
         grads = mm(DP[pl.ds(w * SLAB, SLAB), :], wqkv[...], NT).astype(BF)
         path[w] = mm(back, grads).astype(BF).reshape(path.shape[1:])
         if w == 0:
-            cube_first = to_cube(1, core_first)
+            backs += [
+                remote(path.at[0, :, 3:6], own_path.at[6:18, 0:3], bs.at[0], br.at[0], near(0, 1)),
+                local(path.at[0, :, 0:3], own_path.at[6:18, 3:6], bl.at[0]),
+            ]
+        else:
+            backs += [
+                remote(path.at[1, 0:6, 0:3], own_path.at[18:24, 3:6], bs.at[1], br.at[1], near(0, -1)),
+                remote(path.at[1, 6:12, 0:3], own_path.at[0:6, 3:6], bs.at[2], br.at[2], near(1, -1)),
+                remote(path.at[1, 6:12, 3:6], own_path.at[0:6, 0:3], bs.at[3], br.at[3], near(1, 0)),
+                local(path.at[1, 0:6, 3:6], own_path.at[18:24, 0:3], bl.at[1]),
+            ]
+    cube_first = to_cube(1, core_first)
     cube_second = to_cube(2, core_second)
     take_cube(0, cube_out)
-    backs = [
-        remote(path.at[0, :, 3:6], own_path.at[6:18, 0:3], bs.at[0], br.at[0], near(0, 1)),
-        remote(path.at[1, 0:6, 0:3], own_path.at[18:24, 3:6], bs.at[1], br.at[1], near(0, -1)),
-        remote(path.at[1, 6:12, 0:3], own_path.at[0:6, 3:6], bs.at[2], br.at[2], near(1, -1)),
-        remote(path.at[1, 6:12, 3:6], own_path.at[0:6, 0:3], bs.at[3], br.at[3], near(1, 0)),
-        local(path.at[0, :, 0:3], own_path.at[6:18, 3:6], bl.at[0]),
-        local(path.at[1, 0:6, 3:6], own_path.at[18:24, 0:3], bl.at[1]),
-    ]
     take_cube(1, cube_first)
     far_first = to_far(0)
     take_cube(2, cube_second)

time: 69.6 us -> 74.6 us (1.072)
  Pallas kernels: 64.1 us -> 69 us
    pallas_call x1, Pallas kernels: 64.1 us -> 69 us  [block(): pl.pallas_call(functools.partial(block_kernel, norm), out_shape=(jax.Shap...]
where the time goes in v7:
time: 74.6 us; the launch traced here: 74.3 us
  Pallas kernels  69 us (92%)
  local copies, waits for them, and re-layouts  4.62 us (6%)
    pallas_call x1, Pallas kernels, block(): pl.pallas_call(functools.partial(block_kernel, norm), out_shape=(jax.Shap...  69 us
    unnamed x3, local copies, waits for them, and re-layouts  4.62 us

profile of v7, /device:TPU:1, one launch (start us, length us, event | category | flops | bytes accessed | tf_op | source)
XLA Modules:
  0.0 74.3 jit_solution(1894069829687511908)
XLA Ops:
  0.6 69.0 %block.1 = (bf16[24,6,4,512]{3,2,1,0:T(4,128)(2,1)}, f32[12,128]{1,0:T(8,128)}, f32[4,128]{1,0:T(4,128)}) custom-call(bf16[24,6,4,512]{3,2,1,0:T(4,128)(2,1)} %tok.1, bf16[24,6,4,512]{3,2,1,0:T(4,128)(2,1)} %cot.1, bf16[512,1536]{1,0:T(8,128)(2,1)} %wqkv_in.1, bf16[512,512]{1,0:T(8,128)(2,1)} %wout_in.1), custom_call_target="tpu_custom_call" | custom-call | tf_op jit(solution)/shard_map/block/pallas_call | solution.py:395
  69.7 2.1 %copy.10 = bf16[24,6,4,512]{3,2,1,0:T(4,128)(2,1)} copy(bf16[24,6,4,512]{3,2,1,0:T(4,128)(2,1)} %get-tuple-element.12) | data formatting | bytes 1179648
  71.8 1.3 %copy.11 = f32[1536]{0:T(1024)} copy(f32[1536]{0:T(1024)} %bitcast.2) | data formatting | bytes 12288
  73.1 1.2 %copy.12 = f32[512]{0:T(512)} copy(f32[512]{0:T(512)} %bitcast.3) | data formatting | bytes 4096
